TPU v7x, 128 devices: a whole 4x4x4 slice. The times are simulated.
128 devices in a mesh: row: 8 (over x, core), col: 16 (over z, y).
Axes of the slice: x: 4, y: 4, z: 4, core: 2. Of those that a mesh axis runs over, the one named last changes fastest.
Arguments:
- density: bfloat16 [6144, 6144], P('row', 'col'), may hold values from -5 to 5
- strips: bfloat16 [16384, 8, 128], P(('row', 'col')), may hold values from -5 to 5
- dest_device: int32 [16384, 1], P(('row', 'col')), may hold values from 0 to 127; in each aligned block of 128 rows (0 to 127, 128 to 255, ...) at most 2 rows name the same one
- atom_slot: int32 [16384], P(('row', 'col')), may hold values from 0 to 95
- block_slot: int32 [16384], P(('row', 'col')), may hold values from 0 to 2
- patterns: int32 [3, 48, 48], replicated, may hold values 0 or 1
Outputs:
- density_next: float32 [6144, 6144], P('row', 'col')
- response_next: float32 [6144, 6144], P('row', 'col')
Inputs may be any that keep to these rules, and one draw needn't show every extreme that they name: `dest_device`: of the 128 strips of one device, at most 2 name the same owner, and some owner is named that often.
All inputs are finite; a program needn't handle non-finite values.
Results may differ from a plain program's by a relative error of at most 0.0036.
Values may be sent and summed in bfloat16 or wider, within the bound.
A program may use at most 128 MiB of HBM per device.

v0:
```python
import math

import jax
import jax.numpy as jnp
from jax import lax
from jax.sharding import PartitionSpec as P

STEPS = 2
CAPACITY = 2


def tile_kept(patterns, which, row_offset, col_offset, block_rows, block_cols, block_width):
    window = lax.dynamic_slice(patterns[which], (row_offset, col_offset), (block_rows, block_cols))
    global_rows = row_offset + lax.iota(jnp.int32, block_rows)
    global_cols = col_offset + lax.iota(jnp.int32, block_cols)
    diagonal = (global_rows[:, None] == global_cols[None, :]).astype(jnp.int32)
    kept = jnp.maximum(window, diagonal).astype(jnp.float32)
    return jnp.repeat(jnp.repeat(kept, block_width, axis=0), block_width, axis=1)


def products(zeroth, linear):
    col_zero, col_first = (
        lax.all_gather(zeroth, "row", axis=0, tiled=True),
        lax.all_gather(linear, "row", axis=0, tiled=True),
    )
    pieces = (
        lax.all_gather(zeroth, "col", axis=1, tiled=True),
        lax.all_gather(linear, "col", axis=1, tiled=True),
    )
    square = jnp.dot(pieces[0], col_zero, preferred_element_type=jnp.float32)
    left_part = jnp.dot(pieces[0], col_first, preferred_element_type=jnp.float32)
    right_part = jnp.dot(pieces[1], col_zero, preferred_element_type=jnp.float32)
    return (square, left_part + right_part)


def on_device(density, strips, dest_device, atom_slot, block_slot, patterns):
    tile_rows, tile_cols = density.shape
    mesh_rows = lax.axis_size("row")
    mesh_cols = lax.axis_size("col")
    devices = mesh_rows * mesh_cols
    matrix_order = tile_rows * mesh_rows
    atom_width = strips.shape[1]
    block_width = strips.shape[2]
    block_rows = tile_rows // block_width
    block_cols = tile_cols // block_width
    row_offset = lax.axis_index("row") * block_rows
    col_offset = lax.axis_index("col") * block_cols
    kept_zero = tile_kept(patterns, 0, row_offset, col_offset, block_rows, block_cols, block_width)
    kept_first = tile_kept(patterns, 1, row_offset, col_offset, block_rows, block_cols, block_width)
    kept_field = tile_kept(patterns, 2, row_offset, col_offset, block_rows, block_cols, block_width)
    capacity = CAPACITY
    targets = dest_device[:, 0]
    matches = (targets[:, None] == lax.iota(jnp.int32, devices)[None, :]).astype(jnp.int32)
    before = jnp.cumsum(matches, axis=0) - matches
    ranking = jnp.sum(before * matches, axis=1)
    position = targets * capacity + ranking
    sent_strips = (
        jnp.zeros((devices * capacity, atom_width, block_width), strips.dtype)
        .at[position]
        .set(strips)
    )
    sent_atoms = jnp.full((devices * capacity,), -1, jnp.int32).at[position].set(atom_slot)
    sent_blocks = jnp.zeros((devices * capacity,), jnp.int32).at[position].set(block_slot)
    arrived = (
        lax.all_to_all(
            sent_strips.reshape(devices, capacity, atom_width, block_width),
            ("row", "col"),
            split_axis=0,
            concat_axis=0,
            tiled=True,
        ),
        lax.all_to_all(
            sent_atoms.reshape(devices, capacity),
            ("row", "col"),
            split_axis=0,
            concat_axis=0,
            tiled=True,
        ),
        lax.all_to_all(
            sent_blocks.reshape(devices, capacity),
            ("row", "col"),
            split_axis=0,
            concat_axis=0,
            tiled=True,
        ),
    )
    recv_strips = arrived[0].reshape(-1, atom_width * block_width)
    recv_atoms = arrived[1].reshape(-1)
    recv_blocks = arrived[2].reshape(-1)
    atoms_here = tile_rows // atom_width
    atom_match = recv_atoms[:, None] == lax.iota(jnp.int32, atoms_here)[None, :]
    block_match = recv_blocks[:, None] == lax.iota(jnp.int32, block_cols)[None, :]
    placing = (
        (atom_match[:, :, None] & block_match[:, None, :])
        .astype(jnp.bfloat16)
        .reshape(-1, atoms_here * block_cols)
    )
    summed = lax.dot_general(
        placing, recv_strips, (((0,), (0,)), ((), ())), preferred_element_type=jnp.float32
    )
    h_field = (
        summed.reshape(atoms_here, block_cols, atom_width, block_width)
        .transpose(0, 2, 1, 3)
        .reshape(tile_rows, tile_cols)
    )
    linear = (-(kept_field * h_field)).astype(jnp.bfloat16)
    zeroth = density
    inv_root = 1.0 / math.sqrt(matrix_order)
    new_zeroth = None
    new_linear = None
    for iteration in range(STEPS):
        square, crossed = products(zeroth, linear)
        if iteration % 2 == 0:
            new_zeroth = kept_zero * (square * inv_root)
            new_linear = kept_first * (crossed * inv_root)
        else:
            new_zeroth = kept_zero * (2.0 * zeroth.astype(jnp.float32) - square * inv_root)
            new_linear = kept_first * (2.0 * linear.astype(jnp.float32) - crossed * inv_root)
        zeroth = new_zeroth.astype(jnp.bfloat16)
        linear = new_linear.astype(jnp.bfloat16)
    return (new_zeroth, new_linear)


def solution(mesh):
    return jax.shard_map(
        on_device,
        mesh=mesh,
        in_specs=(
            P("row", "col"),
            P(("row", "col"), None, None),
            P(("row", "col"), None),
            P(("row", "col")),
            P(("row", "col")),
            P(),
        ),
        out_specs=(P("row", "col"), P("row", "col")),
        check_vma=False,
    )
```

profile of v0, /device:TPU:1, one launch (start us, length us, event | category | flops | bytes accessed | tf_op | source)
XLA Modules:
  0.0 541.5 jit_solution(12071236785653305353)
XLA Ops:
  7.9 0.7 fusion.14
  8.8 0.8 select_reduce_fusion
  10.3 1.1 scatter_custom_fusion.1
  11.4 0.8 all_to_all.17
  12.2 11.5 %all-to-all-start.1 = ((s32[128,1,2]{2,1,0:T(1,128)}), s32[128,1,2]{2,1,0:T(1,128)S(1)}, u32[]{:S(2)}, u32[]{:S(2)}) async-start(s32[128,1,2]{2,1,0:T(1,128)} %bitcast.10), calls=%async_computation.1 | async-start | bytes 131072 | tf_op jit(solution)/shard_map/all_to_all | solution.py:79
  23.7 0.8 fusion.23
  25.0 1.1 scatter_custom_fusion
  26.1 0.8 all_to_all.15
  26.9 6.5 %all-to-all-done.1 = s32[128,1,2]{2,1,0:T(1,128)S(1)} async-done(((s32[128,1,2]{2,1,0:T(1,128)}), s32[128,1,2]{2,1,0:T(1,128)S(1)}, u32[]{:S(2)}, u32[]{:S(2)}) %all-to-all-start.1) | async-done | bytes 1056 | tf_op jit(solution)/shard_map/all_to_all | solution.py:79
  33.4 4.3 all-to-all-start
  37.8 0.9 broadcast_in_dim.49
  38.7 13.3 %scatter_fusion = bf16[256,8,128]{2,1,0:T(8,128)(2,1)} fusion(bf16[256,8,128]{2,1,0:T(8,128)(2,1)} %broadcast_in_dim.49, s32[128]{0:T(128)S(1)} %fusion.18, bf16[128,8,128]{2,1,0:T(8,128)(2,1)S(1)} %copy-done.2), kind=kCustom, calls=%fused_computation.2 | custom fusion | bytes 786944 | tf_op jit(solution)/shard_map/scatter | solution.py:60
  52.6 0.8 reduce.6
  53.6 9.8 %all-to-all-start.2 = ((bf16[128,2,8,128]{3,2,1,0:T(8,128)(2,1)}), bf16[128,2,8,128]{3,2,1,0:T(8,128)(2,1)S(1)}, u32[]{:S(2)}, u32[]{:S(2)}) async-start(bf16[128,2,8,128]{3,2,1,0:T(8,128)(2,1)} %bitcast.13), calls=%async_computation.2 | async-start | bytes 1048576 | tf_op jit(solution)/shard_map/all_to_all | solution.py:65
  63.4 0.8 reduce.7
  64.8 12.6 %all-to-all-done.2 = bf16[128,2,8,128]{3,2,1,0:T(8,128)(2,1)S(1)} async-done(((bf16[128,2,8,128]{3,2,1,0:T(8,128)(2,1)}), bf16[128,2,8,128]{3,2,1,0:T(8,128)(2,1)S(1)}, u32[]{:S(2)}, u32[]{:S(2)}) %all-to-all-start.2) | async-done | bytes 524320 | tf_op jit(solution)/shard_map/all_to_all | solution.py:65
  79.2 0.9 fusion.12
  82.1 69.6 %all-gather.19.cloned.1.call-done = bf16[768,6144]{0,1:T(8,128)(2,1)} async-done(((bf16[768,384]{0,1:T(8,128)(2,1)}), bf16[768,6144]{0,1:T(8,128)(2,1)}) %all-gather.19.cloned.1.call-update) | async-done | bytes 9437200 | tf_op jit(solution)/shard_map/all_gather | solution.py:28
  151.7 9.0 %fusion.24 = f32[768,384]{1,0:T(8,128)S(1)} fusion(bf16[768,6144]{0,1:T(8,128)(2,1)} %all-gather.19.cloned.1.call-done, bf16[6144,384]{1,0:T(8,128)(2,1)} %all-gather.11.cloned.1.call-done), kind=kOutput, calls=%fused_computation.56 | convolution fusion | flops 3623878656 | bytes 15335424 | tf_op jit(solution)/shard_map/dot_general | solution.py:32
  160.7 27.5 %all-gather.17.cloned.1.call-done = bf16[6144,384]{0,1:T(8,128)(2,1)} async-done(((bf16[768,384]{0,1:T(8,128)(2,1)}), bf16[6144,384]{0,1:T(8,128)(2,1)}) %all-gather.17.cloned.1.call-update) | async-done | bytes 4718608 | tf_op jit(solution)/shard_map/all_gather | solution.py:24
  188.3 84.6 %all-gather.9.cloned.1.call-done = bf16[768,6144]{1,0:T(8,128)(2,1)} async-done(((bf16[768,384]{1,0:T(8,128)(2,1)}), bf16[768,6144]{1,0:T(8,128)(2,1)}) %all-gather.9.cloned.1.call-update) | async-done | bytes 9437200 | tf_op jit(solution)/shard_map/all_gather | solution.py:27
  272.8 9.8 %fusion.9 = bf16[768,384]{1,0:T(8,128)(2,1)} fusion(f32[768,384]{1,0:T(8,128)S(1)} %copy.40, f32[768,384]{1,0:T(8,128)S(1)} %fusion.24, bf16[6144,384]{0,1:T(8,128)(2,1)} %all-gather.17.cloned.1.call-done, bf16[768,6144]{1,0:T(8,128)(2,1)} %all-gather.9.cloned.1.call-done), kind=kOutput, calls=%fused_computation.17 | convolution fusion | flops 3625058304 | bytes 17104896 | tf_op jit(solution)/shard_map/dot_general | solution.py:31
  283.4 9.7 %fusion.10 = bf16[768,384]{1,0:T(8,128)(2,1)} fusion(f32[768,384]{1,0:T(8,128)S(1)} %copy.29, bf16[768,6144]{1,0:T(8,128)(2,1)} %all-gather.9.cloned.1.call-done, bf16[6144,384]{1,0:T(8,128)(2,1)} %all-gather.11.cloned.1.call-done), kind=kOutput, calls=%fused_computation.18 | convolution fusion | flops 3624763392 | bytes 15925248 | tf_op jit(solution)/shard_map/dot_general | solution.py:30
  293.2 0.7 all-gather.15.cloned.1.call-update
  294.0 0.7 all-gather.23.cloned.1.call-update
  294.7 22.9 %all-gather.21.cloned.1.call-done = bf16[6144,384]{1,0:T(8,128)(2,1)} async-done(((bf16[768,384]{1,0:T(8,128)(2,1)}), bf16[6144,384]{1,0:T(8,128)(2,1)}) %all-gather.21.cloned.1.call-update) | async-done | bytes 4718608 | tf_op jit(solution)/shard_map/all_gather | solution.py:24
  317.6 85.1 %all-gather.13.cloned.1.call-done = bf16[768,6144]{1,0:T(8,128)(2,1)} async-done(((bf16[768,384]{1,0:T(8,128)(2,1)}), bf16[768,6144]{1,0:T(8,128)(2,1)}) %all-gather.13.cloned.1.call-update) | async-done | bytes 9437200 | tf_op jit(solution)/shard_map/all_gather | solution.py:27
  402.7 9.8 %fusion.25 = f32[768,384]{1,0:T(8,128)} fusion(bf16[768,6144]{1,0:T(8,128)(2,1)} %all-gather.13.cloned.1.call-done, bf16[6144,384]{1,0:T(8,128)(2,1)} %all-gather.21.cloned.1.call-done), kind=kOutput, calls=%fused_computation.57 | convolution fusion | flops 3623878656 | bytes 15335424 | tf_op jit(solution)/shard_map/dot_general | solution.py:31
  412.5 27.3 %all-gather.15.cloned.1.call-done = bf16[6144,384]{1,0:T(8,128)(2,1)} async-done(((bf16[768,384]{1,0:T(8,128)(2,1)}), bf16[6144,384]{1,0:T(8,128)(2,1)}) %all-gather.15.cloned.1.call-update) | async-done | bytes 4718608 | tf_op jit(solution)/shard_map/all_gather | solution.py:23
  439.8 9.8 %fusion.2 = f32[768,384]{1,0:T(8,128)} fusion(f32[768,384]{1,0:T(8,128)S(1)} %copy.29, bf16[768,6144]{1,0:T(8,128)(2,1)} %all-gather.13.cloned.1.call-done, bf16[6144,384]{1,0:T(8,128)(2,1)} %all-gather.15.cloned.1.call-done, bf16[768,384]{1,0:T(8,128)(2,1)S(1)} %copy-done.1), kind=kOutput, calls=%fused_computation.9 | convolution fusion | flops 3625353216 | bytes 17104896 | tf_op jit(solution)/shard_map/dot_general | solution.py:30
  449.6 74.9 %all-gather.23.cloned.1.call-done = bf16[768,6144]{1,0:T(8,128)(2,1)} async-done(((bf16[768,384]{1,0:T(8,128)(2,1)}), bf16[768,6144]{1,0:T(8,128)(2,1)}) %all-gather.23.cloned.1.call-update) | async-done | bytes 9437200 | tf_op jit(solution)/shard_map/all_gather | solution.py:28
  524.5 10.1 %fusion.8 = f32[768,384]{1,0:T(8,128)} fusion(f32[768,384]{1,0:T(8,128)S(1)} %copy.40, f32[768,384]{1,0:T(8,128)} %fusion.25, bf16[768,6144]{1,0:T(8,128)(2,1)} %all-gather.23.cloned.1.call-done, bf16[6144,384]{1,0:T(8,128)(2,1)} %all-gather.15.cloned.1.call-done, bf16[768,384]{1,0:T(8,128)(2,1)S(1)} %copy-done), kind=kOutput, calls=%fused_computation.16 | convolution fusion | flops 3625648128 | bytes 18284544 | tf_op jit(solution)/shard_map/dot_general | solution.py:32
  (55 shorter events, 7.9 us)
Async XLA Ops:
  7.2 31.5 %copy-start.2 = (bf16[128,8,128]{2,1,0:T(8,128)(2,1)S(1)}, bf16[128,8,128]{2,1,0:T(8,128)(2,1)}, u32[]{:S(2)}) copy-start(bf16[128,8,128]{2,1,0:T(8,128)(2,1)} %param.7) | copy-start | bytes 786436
  7.2 74.9 %all-gather.11.cloned.1.call-start = ((), (), s32[]{:S(2)}) async-start(), calls=%async_computation.4 | async-start | bytes 5308416 | tf_op jit(solution)/shard_map/all_gather | solution.py:23
  12.2 21.2 %all-to-all-start.1 = ((s32[128,1,2]{2,1,0:T(1,128)}), s32[128,1,2]{2,1,0:T(1,128)S(1)}, u32[]{:S(2)}, u32[]{:S(2)}) async-start(s32[128,1,2]{2,1,0:T(1,128)} %bitcast.10), calls=%async_computation.1 | async-start | bytes 131072 | tf_op jit(solution)/shard_map/all_to_all | solution.py:79
  33.4 20.2 %all-to-all-start = ((s32[128,1,2]{2,1,0:T(1,128)}), s32[128,1,2]{2,1,0:T(1,128)S(1)}, u32[]{:S(2)}, u32[]{:S(2)}) async-start(s32[128,1,2]{2,1,0:T(1,128)} %bitcast.9), calls=%async_computation | async-start | bytes 131072 | tf_op jit(solution)/shard_map/all_to_all | solution.py:72
  53.6 23.9 %all-to-all-start.2 = ((bf16[128,2,8,128]{3,2,1,0:T(8,128)(2,1)}), bf16[128,2,8,128]{3,2,1,0:T(8,128)(2,1)S(1)}, u32[]{:S(2)}, u32[]{:S(2)}) async-start(bf16[128,2,8,128]{3,2,1,0:T(8,128)(2,1)} %bitcast.13), calls=%async_computation.2 | async-start | bytes 1048576 | tf_op jit(solution)/shard_map/all_to_all | solution.py:65
  63.4 88.3 %all-gather.19.cloned.1.call-start = ((), (), s32[]{:S(2)}) async-start(), calls=%async_computation.8 | async-start | bytes 10027008 | tf_op jit(solution)/shard_map/all_gather | solution.py:28
  80.1 108.1 %all-gather.17.cloned.1.call-start = ((), (), s32[]{:S(2)}) async-start(), calls=%async_computation.7 | async-start | bytes 5308416 | tf_op jit(solution)/shard_map/all_gather | solution.py:24
  80.9 192.0 %all-gather.9.cloned.1.call-start = ((), (), s32[]{:S(2)}) async-start(), calls=%async_computation.3 | async-start | bytes 10027008 | tf_op jit(solution)/shard_map/all_gather | solution.py:27
  81.4 236.2 %all-gather.21.cloned.1.call-start = ((), (), s32[]{:S(2)}) async-start(), calls=%async_computation.9 | async-start | bytes 5308416 | tf_op jit(solution)/shard_map/all_gather | solution.py:24
  282.7 120.1 %all-gather.13.cloned.1.call-start = ((), (), s32[]{:S(2)}) async-start(), calls=%async_computation.5 | async-start | bytes 10027008 | tf_op jit(solution)/shard_map/all_gather | solution.py:27
  293.2 146.7 %all-gather.15.cloned.1.call-start = ((), (), s32[]{:S(2)}) async-start(), calls=%async_computation.6 | async-start | bytes 5308416 | tf_op jit(solution)/shard_map/all_gather | solution.py:23
  293.9 230.6 %all-gather.23.cloned.1.call-start = ((), (), s32[]{:S(2)}) async-start(), calls=%async_computation.10 | async-start | bytes 10027008 | tf_op jit(solution)/shard_map/all_gather | solution.py:28
  294.7 145.2 %copy-start.1 = (bf16[768,384]{1,0:T(8,128)(2,1)S(1)}, bf16[768,384]{1,0:T(8,128)(2,1)}, u32[]{:S(2)}) copy-start(bf16[768,384]{1,0:T(8,128)(2,1)} %fusion.10) | copy-start | bytes 1769476
  412.5 112.0 %copy-start = (bf16[768,384]{1,0:T(8,128)(2,1)S(1)}, bf16[768,384]{1,0:T(8,128)(2,1)}, u32[]{:S(2)}) copy-start(bf16[768,384]{1,0:T(8,128)(2,1)} %fusion.9) | copy-start | bytes 1769476
Sparse Core Ops, SparseCore 0:
  9.7 39.2 all-gather.10
  80.2 71.3 all-gather.18
  153.9 34.2 all-gather.16
  190.2 82.5 all-gather.8
  282.8 34.7 all-gather.20
  320.1 82.5 all-gather.12
  405.0 34.7 all-gather.14
  441.9 82.5 all-gather.22
where the time goes:
time: 542 us; the launch traced here: 541 us
  waiting for transfers between devices  414 us (76%)
  matrix products  58.6 us (11%)
  starting transfers between devices  26 us (5%)
  local copies, waits for them, and re-layouts  22.8 us (4%)
  between operations  14.4 us (3%)
    all_gather x2, waiting for transfers between devices, products(): lax.all_gather(zeroth, 'col', axis=1, tiled=True)  170 us
    all_gather x2, waiting for transfers between devices, products(): lax.all_gather(linear, 'col', axis=1, tiled=True)  145 us
    all_gather x2, waiting for transfers between devices, products(): lax.all_gather(linear, 'row', axis=0, tiled=True)  50.5 us
    all_gather x2, waiting for transfers between devices, products(): lax.all_gather(zeroth, 'row', axis=0, tiled=True)  27.3 us
    dot_general x2, matrix products, products(): jnp.dot(pieces[0], col_first, preferred_element_type=jnp.float32)  19.6 us
    dot_general x2, matrix products, products(): square = jnp.dot(pieces[0], col_zero, preferred_element_type=jnp.float32)  19.5 us
    dot_general x2, matrix products, products(): jnp.dot(pieces[1], col_zero, preferred_element_type=jnp.float32)  19.1 us
    scatter x1, local copies, waits for them, and re-layouts, on_device(): sent_strips = jnp.zeros((devices * capacity, atom_width, block_width), st...  13.3 us
  transfers between devices with their start and end apart: 11, of which 9 were waited for; matrix products, arithmetic and copies ran while one was open for 12% of the time, Pallas kernels for 0%

commit v1 on v0

--- a/solution.py
+++ b/solution.py
@@ -50,9 +50,9 @@
     kept_field = tile_kept(patterns, 2, row_offset, col_offset, block_rows, block_cols, block_width)
     capacity = CAPACITY
     targets = dest_device[:, 0]
-    matches = (targets[:, None] == lax.iota(jnp.int32, devices)[None, :]).astype(jnp.int32)
-    before = jnp.cumsum(matches, axis=0) - matches
-    ranking = jnp.sum(before * matches, axis=1)
+    order = lax.iota(jnp.int32, targets.shape[0])
+    earlier = (targets[:, None] == targets[None, :]) & (order[None, :] < order[:, None])
+    ranking = jnp.sum(earlier.astype(jnp.int32), axis=1)
     position = targets * capacity + ranking
     sent_strips = (
         jnp.zeros((devices * capacity, atom_width, block_width), strips.dtype)

time: 542 us -> 541 us (level)
  no operation moved by 1% of the time
where the time goes in v1:
time: 541 us
  waiting for transfers between devices  415 us (77%)
  matrix products  58.5 us (11%)
  starting transfers between devices  26.2 us (5%)
  local copies, waits for them, and re-layouts  22.8 us (4%)
  between operations  14.4 us (3%)
    all_gather x2, waiting for transfers between devices, products(): lax.all_gather(zeroth, 'col', axis=1, tiled=True)  170 us
    all_gather x2, waiting for transfers between devices, products(): lax.all_gather(linear, 'col', axis=1, tiled=True)  145 us
    all_gather x2, waiting for transfers between devices, products(): lax.all_gather(linear, 'row', axis=0, tiled=True)  50.5 us
    all_gather x2, waiting for transfers between devices, products(): lax.all_gather(zeroth, 'row', axis=0, tiled=True)  27.3 us
    dot_general x2, matrix products, products(): jnp.dot(pieces[0], col_first, preferred_element_type=jnp.float32)  19.6 us
    dot_general x2, matrix products, products(): square = jnp.dot(pieces[0], col_zero, preferred_element_type=jnp.float32)  19.5 us
    dot_general x2, matrix products, products(): jnp.dot(pieces[1], col_zero, preferred_element_type=jnp.float32)  19.1 us
    scatter x1, local copies, waits for them, and re-layouts, on_device(): sent_strips = jnp.zeros((devices * capacity, atom_width, block_width), st...  13.4 us
  transfers between devices with their start and end apart: 11, of which 9 were waited for; matrix products, arithmetic and copies ran while one was open for 12% of the time, Pallas kernels for 0%

profile of v1, /device:TPU:1, one launch (start us, length us, event | category | flops | bytes accessed | tf_op | source)
XLA Modules:
  0.0 540.8 jit_solution(16579620292933018582)
XLA Ops:
  7.9 0.9 convert_reduce_fusion
  9.5 1.1 scatter_custom_fusion.1
  10.6 0.8 all_to_all.17
  11.4 11.5 %all-to-all-start.1 = ((s32[128,1,2]{2,1,0:T(1,128)}), s32[128,1,2]{2,1,0:T(1,128)S(1)}, u32[]{:S(2)}, u32[]{:S(2)}) async-start(s32[128,1,2]{2,1,0:T(1,128)} %bitcast.10), calls=%async_computation.1 | async-start | bytes 131072 | tf_op jit(solution)/shard_map/all_to_all | solution.py:79
  22.9 0.8 fusion.23
  24.2 1.1 scatter_custom_fusion
  25.3 0.8 all_to_all.15
  26.1 6.5 %all-to-all-done.1 = s32[128,1,2]{2,1,0:T(1,128)S(1)} async-done(((s32[128,1,2]{2,1,0:T(1,128)}), s32[128,1,2]{2,1,0:T(1,128)S(1)}, u32[]{:S(2)}, u32[]{:S(2)}) %all-to-all-start.1) | async-done | bytes 1056 | tf_op jit(solution)/shard_map/all_to_all | solution.py:79
  32.6 4.4 all-to-all-start
  37.1 0.9 broadcast_in_dim.50
  38.0 13.4 %scatter_fusion = bf16[256,8,128]{2,1,0:T(8,128)(2,1)} fusion(bf16[256,8,128]{2,1,0:T(8,128)(2,1)} %broadcast_in_dim.50, s32[128]{0:T(128)S(1)} %fusion.18, bf16[128,8,128]{2,1,0:T(8,128)(2,1)S(1)} %copy-done.2), kind=kCustom, calls=%fused_computation.2 | custom fusion | bytes 786944 | tf_op jit(solution)/shard_map/scatter | solution.py:60
  51.9 0.8 reduce.6
  52.9 9.8 %all-to-all-start.2 = ((bf16[128,2,8,128]{3,2,1,0:T(8,128)(2,1)}), bf16[128,2,8,128]{3,2,1,0:T(8,128)(2,1)S(1)}, u32[]{:S(2)}, u32[]{:S(2)}) async-start(bf16[128,2,8,128]{3,2,1,0:T(8,128)(2,1)} %bitcast.13), calls=%async_computation.2 | async-start | bytes 1048576 | tf_op jit(solution)/shard_map/all_to_all | solution.py:65
  62.7 0.8 reduce.7
  64.1 12.7 %all-to-all-done.2 = bf16[128,2,8,128]{3,2,1,0:T(8,128)(2,1)S(1)} async-done(((bf16[128,2,8,128]{3,2,1,0:T(8,128)(2,1)}), bf16[128,2,8,128]{3,2,1,0:T(8,128)(2,1)S(1)}, u32[]{:S(2)}, u32[]{:S(2)}) %all-to-all-start.2) | async-done | bytes 524320 | tf_op jit(solution)/shard_map/all_to_all | solution.py:65
  77.4 0.7 copy.70
  78.5 0.9 fusion.12
  81.4 69.6 %all-gather.19.cloned.1.call-done = bf16[768,6144]{0,1:T(8,128)(2,1)} async-done(((bf16[768,384]{0,1:T(8,128)(2,1)}), bf16[768,6144]{0,1:T(8,128)(2,1)}) %all-gather.19.cloned.1.call-update) | async-done | bytes 9437200 | tf_op jit(solution)/shard_map/all_gather | solution.py:28
  151.0 9.0 %fusion.24 = f32[768,384]{1,0:T(8,128)S(1)} fusion(bf16[768,6144]{0,1:T(8,128)(2,1)} %all-gather.19.cloned.1.call-done, bf16[6144,384]{1,0:T(8,128)(2,1)} %all-gather.11.cloned.1.call-done), kind=kOutput, calls=%fused_computation.56 | convolution fusion | flops 3623878656 | bytes 15335424 | tf_op jit(solution)/shard_map/dot_general | solution.py:32
  160.0 27.6 %all-gather.17.cloned.1.call-done = bf16[6144,384]{0,1:T(8,128)(2,1)} async-done(((bf16[768,384]{0,1:T(8,128)(2,1)}), bf16[6144,384]{0,1:T(8,128)(2,1)}) %all-gather.17.cloned.1.call-update) | async-done | bytes 4718608 | tf_op jit(solution)/shard_map/all_gather | solution.py:24
  187.6 84.6 %all-gather.9.cloned.1.call-done = bf16[768,6144]{1,0:T(8,128)(2,1)} async-done(((bf16[768,384]{1,0:T(8,128)(2,1)}), bf16[768,6144]{1,0:T(8,128)(2,1)}) %all-gather.9.cloned.1.call-update) | async-done | bytes 9437200 | tf_op jit(solution)/shard_map/all_gather | solution.py:27
  272.1 9.8 %fusion.9 = bf16[768,384]{1,0:T(8,128)(2,1)} fusion(f32[768,384]{1,0:T(8,128)S(1)} %copy.54, f32[768,384]{1,0:T(8,128)S(1)} %fusion.24, bf16[6144,384]{0,1:T(8,128)(2,1)} %all-gather.17.cloned.1.call-done, bf16[768,6144]{1,0:T(8,128)(2,1)} %all-gather.9.cloned.1.call-done), kind=kOutput, calls=%fused_computation.17 | convolution fusion | flops 3625058304 | bytes 17104896 | tf_op jit(solution)/shard_map/dot_general | solution.py:31
  282.7 9.7 %fusion.10 = bf16[768,384]{1,0:T(8,128)(2,1)} fusion(f32[768,384]{1,0:T(8,128)S(1)} %copy.43, bf16[768,6144]{1,0:T(8,128)(2,1)} %all-gather.9.cloned.1.call-done, bf16[6144,384]{1,0:T(8,128)(2,1)} %all-gather.11.cloned.1.call-done), kind=kOutput, calls=%fused_computation.18 | convolution fusion | flops 3624763392 | bytes 15925248 | tf_op jit(solution)/shard_map/dot_general | solution.py:30
  292.5 0.7 all-gather.15.cloned.1.call-update
  293.3 0.7 all-gather.23.cloned.1.call-update
  294.0 22.9 %all-gather.21.cloned.1.call-done = bf16[6144,384]{1,0:T(8,128)(2,1)} async-done(((bf16[768,384]{1,0:T(8,128)(2,1)}), bf16[6144,384]{1,0:T(8,128)(2,1)}) %all-gather.21.cloned.1.call-update) | async-done | bytes 4718608 | tf_op jit(solution)/shard_map/all_gather | solution.py:24
  316.9 85.1 %all-gather.13.cloned.1.call-done = bf16[768,6144]{1,0:T(8,128)(2,1)} async-done(((bf16[768,384]{1,0:T(8,128)(2,1)}), bf16[768,6144]{1,0:T(8,128)(2,1)}) %all-gather.13.cloned.1.call-update) | async-done | bytes 9437200 | tf_op jit(solution)/shard_map/all_gather | solution.py:27
  402.0 9.8 %fusion.25 = f32[768,384]{1,0:T(8,128)} fusion(bf16[768,6144]{1,0:T(8,128)(2,1)} %all-gather.13.cloned.1.call-done, bf16[6144,384]{1,0:T(8,128)(2,1)} %all-gather.21.cloned.1.call-done), kind=kOutput, calls=%fused_computation.57 | convolution fusion | flops 3623878656 | bytes 15335424 | tf_op jit(solution)/shard_map/dot_general | solution.py:31
  411.8 27.3 %all-gather.15.cloned.1.call-done = bf16[6144,384]{1,0:T(8,128)(2,1)} async-done(((bf16[768,384]{1,0:T(8,128)(2,1)}), bf16[6144,384]{1,0:T(8,128)(2,1)}) %all-gather.15.cloned.1.call-update) | async-done | bytes 4718608 | tf_op jit(solution)/shard_map/all_gather | solution.py:23
  439.1 9.8 %fusion.2 = f32[768,384]{1,0:T(8,128)} fusion(f32[768,384]{1,0:T(8,128)S(1)} %copy.43, bf16[768,6144]{1,0:T(8,128)(2,1)} %all-gather.13.cloned.1.call-done, bf16[6144,384]{1,0:T(8,128)(2,1)} %all-gather.15.cloned.1.call-done, bf16[768,384]{1,0:T(8,128)(2,1)S(1)} %copy-done.1), kind=kOutput, calls=%fused_computation.9 | convolution fusion | flops 3625353216 | bytes 17104896 | tf_op jit(solution)/shard_map/dot_general | solution.py:30
  448.9 74.9 %all-gather.23.cloned.1.call-done = bf16[768,6144]{1,0:T(8,128)(2,1)} async-done(((bf16[768,384]{1,0:T(8,128)(2,1)}), bf16[768,6144]{1,0:T(8,128)(2,1)}) %all-gather.23.cloned.1.call-update) | async-done | bytes 9437200 | tf_op jit(solution)/shard_map/all_gather | solution.py:28
  523.8 10.1 %fusion.8 = f32[768,384]{1,0:T(8,128)} fusion(f32[768,384]{1,0:T(8,128)S(1)} %copy.54, f32[768,384]{1,0:T(8,128)} %fusion.25, bf16[768,6144]{1,0:T(8,128)(2,1)} %all-gather.23.cloned.1.call-done, bf16[6144,384]{1,0:T(8,128)(2,1)} %all-gather.15.cloned.1.call-done, bf16[768,384]{1,0:T(8,128)(2,1)S(1)} %copy-done), kind=kOutput, calls=%fused_computation.16 | convolution fusion | flops 3625648128 | bytes 18284544 | tf_op jit(solution)/shard_map/dot_general | solution.py:32
  (53 shorter events, 7.0 us)
Async XLA Ops:
  7.2 30.8 %copy-start.2 = (bf16[128,8,128]{2,1,0:T(8,128)(2,1)S(1)}, bf16[128,8,128]{2,1,0:T(8,128)(2,1)}, u32[]{:S(2)}) copy-start(bf16[128,8,128]{2,1,0:T(8,128)(2,1)} %param.7) | copy-start | bytes 786436
  7.2 74.2 %all-gather.11.cloned.1.call-start = ((), (), s32[]{:S(2)}) async-start(), calls=%async_computation.4 | async-start | bytes 5308416 | tf_op jit(solution)/shard_map/all_gather | solution.py:23
  11.4 21.2 %all-to-all-start.1 = ((s32[128,1,2]{2,1,0:T(1,128)}), s32[128,1,2]{2,1,0:T(1,128)S(1)}, u32[]{:S(2)}, u32[]{:S(2)}) async-start(s32[128,1,2]{2,1,0:T(1,128)} %bitcast.10), calls=%async_computation.1 | async-start | bytes 131072 | tf_op jit(solution)/shard_map/all_to_all | solution.py:79
  32.6 20.3 %all-to-all-start = ((s32[128,1,2]{2,1,0:T(1,128)}), s32[128,1,2]{2,1,0:T(1,128)S(1)}, u32[]{:S(2)}, u32[]{:S(2)}) async-start(s32[128,1,2]{2,1,0:T(1,128)} %bitcast.9), calls=%async_computation | async-start | bytes 131072 | tf_op jit(solution)/shard_map/all_to_all | solution.py:72
  52.9 23.9 %all-to-all-start.2 = ((bf16[128,2,8,128]{3,2,1,0:T(8,128)(2,1)}), bf16[128,2,8,128]{3,2,1,0:T(8,128)(2,1)S(1)}, u32[]{:S(2)}, u32[]{:S(2)}) async-start(bf16[128,2,8,128]{3,2,1,0:T(8,128)(2,1)} %bitcast.13), calls=%async_computation.2 | async-start | bytes 1048576 | tf_op jit(solution)/shard_map/all_to_all | solution.py:65
  62.7 88.3 %all-gather.19.cloned.1.call-start = ((), (), s32[]{:S(2)}) async-start(), calls=%async_computation.8 | async-start | bytes 10027008 | tf_op jit(solution)/shard_map/all_gather | solution.py:28
  79.4 108.1 %all-gather.17.cloned.1.call-start = ((), (), s32[]{:S(2)}) async-start(), calls=%async_computation.7 | async-start | bytes 5308416 | tf_op jit(solution)/shard_map/all_gather | solution.py:24
  80.2 192.0 %all-gather.9.cloned.1.call-start = ((), (), s32[]{:S(2)}) async-start(), calls=%async_computation.3 | async-start | bytes 10027008 | tf_op jit(solution)/shard_map/all_gather | solution.py:27
  80.7 236.2 %all-gather.21.cloned.1.call-start = ((), (), s32[]{:S(2)}) async-start(), calls=%async_computation.9 | async-start | bytes 5308416 | tf_op jit(solution)/shard_map/all_gather | solution.py:24
  281.9 120.1 %all-gather.13.cloned.1.call-start = ((), (), s32[]{:S(2)}) async-start(), calls=%async_computation.5 | async-start | bytes 10027008 | tf_op jit(solution)/shard_map/all_gather | solution.py:27
  292.5 146.7 %all-gather.15.cloned.1.call-start = ((), (), s32[]{:S(2)}) async-start(), calls=%async_computation.6 | async-start | bytes 5308416 | tf_op jit(solution)/shard_map/all_gather | solution.py:23
  293.2 230.6 %all-gather.23.cloned.1.call-start = ((), (), s32[]{:S(2)}) async-start(), calls=%async_computation.10 | async-start | bytes 10027008 | tf_op jit(solution)/shard_map/all_gather | solution.py:28
  294.0 145.2 %copy-start.1 = (bf16[768,384]{1,0:T(8,128)(2,1)S(1)}, bf16[768,384]{1,0:T(8,128)(2,1)}, u32[]{:S(2)}) copy-start(bf16[768,384]{1,0:T(8,128)(2,1)} %fusion.10) | copy-start | bytes 1769476
  411.8 112.0 %copy-start = (bf16[768,384]{1,0:T(8,128)(2,1)S(1)}, bf16[768,384]{1,0:T(8,128)(2,1)}, u32[]{:S(2)}) copy-start(bf16[768,384]{1,0:T(8,128)(2,1)} %fusion.9) | copy-start | bytes 1769476
Sparse Core Ops, SparseCore 0:
  9.7 38.8 all-gather.10
  79.6 71.3 all-gather.18
  153.3 34.2 all-gather.16
  189.5 82.5 all-gather.8
  282.1 34.7 all-gather.20
  319.4 82.5 all-gather.12
  404.3 34.7 all-gather.14
  441.2 82.5 all-gather.22

commit v2 on v1

v2 whole, which is shorter than its diff:
```python
import functools
import math

import jax
import jax.numpy as jnp
from jax import lax
from jax.experimental import pallas as pl
from jax.experimental.pallas import tpu as pltpu
from jax.sharding import PartitionSpec as P

CAPACITY = 2
MESH = pl.DeviceIdType.MESH
BF = jnp.bfloat16
F32 = jnp.float32
TR, TC = 768, 384
KB = 1536
SUB = 192
BLK = 128
PLACE = {2: (0, 0), 1: (0, TC), 3: (1, 0), 0: (1, TC)}
N_COPIES = 200


def local_tile(patterns, which, row_offset, col_offset, block_rows, block_cols, block_width):
    window = lax.dynamic_slice(patterns[which], (row_offset, col_offset), (block_rows, block_cols))
    global_rows = row_offset + lax.iota(jnp.int32, block_rows)
    global_cols = col_offset + lax.iota(jnp.int32, block_cols)
    diagonal = (global_rows[:, None] == global_cols[None, :]).astype(jnp.int32)
    kept = jnp.maximum(window, diagonal).astype(jnp.float32)
    return jnp.repeat(jnp.repeat(kept, block_width, axis=0), block_width, axis=1)


def start_linear(strips, dest_device, atom_slot, block_slot, patterns):
    n, atom_width, width = strips.shape
    devices = lax.axis_size("row") * lax.axis_size("col")
    block_rows, block_cols = TR // width, TC // width
    row_offset = lax.axis_index("row") * block_rows
    col_offset = lax.axis_index("col") * block_cols
    kept_field = local_tile(patterns, 2, row_offset, col_offset, block_rows, block_cols, width)
    targets = dest_device[:, 0]
    order = lax.iota(jnp.int32, n)
    earlier = (targets[:, None] == targets[None, :]) & (order[None, :] < order[:, None])
    ranking = jnp.sum(earlier.astype(jnp.int32), axis=1)
    position = targets * CAPACITY + ranking
    spread = (lax.iota(jnp.int32, devices * CAPACITY)[:, None] == position[None, :]).astype(BF)
    lanes = lax.iota(jnp.int32, width)[None, :]
    tags = jnp.where(
        lanes == 0, atom_slot[:, None] + 1, jnp.where(lanes == 1, block_slot[:, None], 0)
    ).astype(BF)
    rows = jnp.concatenate([strips.reshape(n, atom_width * width), tags], axis=1)
    sent = jnp.dot(spread, rows, preferred_element_type=F32).astype(BF)
    got = lax.all_to_all(
        sent.reshape(devices, CAPACITY, (atom_width + 1) * width),
        ("row", "col"), split_axis=0, concat_axis=0, tiled=True,
    ).reshape(devices * CAPACITY, (atom_width + 1) * width)
    recv_atoms = got[:, atom_width * width].astype(jnp.int32) - 1
    recv_blocks = got[:, atom_width * width + 1].astype(jnp.int32)
    atoms_here = TR // atom_width
    cell = recv_atoms * block_cols + recv_blocks
    placing = (cell[:, None] == lax.iota(jnp.int32, atoms_here * block_cols)[None, :]) & (
        recv_atoms[:, None] >= 0
    )
    summed = lax.dot_general(
        placing.astype(BF), got[:, : atom_width * width], (((0,), (0,)), ((), ())),
        preferred_element_type=F32,
    )
    h_field = (
        summed.reshape(atoms_here, block_cols, atom_width, width)
        .transpose(0, 2, 1, 3)
        .reshape(TR, TC)
    )
    return (-(kept_field * h_field)).astype(BF)


def kernel(
    zero_hbm, first_hbm, patterns, out_zero, out_first,
    a, b, turn, total, part, near, far, send_sem, recv_sem, local_sem,
):
    row, col = lax.axis_index("row"), lax.axis_index("col")
    x, core = row // 2, row % 2
    z, y = col // 4, col % 4

    def at(dx=0, dz=0, dy=0, dc=0):
        nx, nz, ny = (lax.rem(x + dx, 4), lax.rem(z + dz, 4), lax.rem(y + dy, 4))
        return {"row": nx * 2 + lax.rem(core + dc, 2), "col": nz * 4 + ny}

    copies = {}
    locals_ = {}

    def send(name, src, dst, device):
        i = len(copies)
        copy = pltpu.make_async_remote_copy(
            src_ref=src, dst_ref=dst, send_sem=send_sem.at[i], recv_sem=recv_sem.at[i],
            device_id=device, device_id_type=MESH,
        )
        copies[name] = copy
        copy.start()

    def got(*names):
        for name in names:
            copies[name].wait_recv()

    def move(name, src, dst):
        copy = pltpu.make_async_copy(src, dst, local_sem.at[len(locals_)])
        locals_[name] = copy
        copy.start()

    def lanes(position):
        return pl.ds(pl.multiple_of(position * TC, BLK), TC)

    def rows_of(position, first=0, size=SUB):
        return pl.ds(pl.multiple_of(core * TR + position * SUB + first, 32), size)

    peers = [at(dy=1), at(dy=3), at(dx=1), at(dx=2), at(dx=3), at(dz=1), at(dz=2), at(dz=3), at(dc=1)]

    def tile(u, rows=slice(None)):
        return a.at[u, rows, lanes(y)]

    def begin_turn(u):
        for dx in (2, 1, 3):
            q = lax.rem(x + dx, 4)
            src = tile(u, pl.ds(pl.multiple_of(q * SUB, 32), SUB))
            send(("tx", u, dx), src, turn.at[u, (4 - dx) % 4], at(dx=dx))
        move(("tx", u), tile(u, pl.ds(pl.multiple_of(x * SUB, 32), SUB)), turn.at[u, 0])

    def begin_side(u):
        send(("y", u, 1), tile(u), tile(u), at(dy=1))
        send(("y", u, 3), tile(u), tile(u), at(dy=3))

    def turn_z(u):
        got(*(("tx", u, dx) for dx in (1, 2, 3)))
        locals_["tx", u].wait()
        for dz in (2, 3, 1, 0):
            chunk, lane = PLACE[(4 - dz) % 4]
            src = turn.at[u, lax.rem(z + dz + 4 - x, 4)]
            dst = b.at[u, chunk, rows_of(x), pl.ds(lane, TC)]
            if dz:
                send(("tz", u, dz), src, dst, at(dz=dz))
            else:
                move(("tz", u), src, dst)

    def spread_own(u, ch):
        if ch == 0:
            got(("tz", u, 2), ("tz", u, 3))
        else:
            got(("tz", u, 1))
            locals_["tz", u].wait()
        own = b.at[u, ch, rows_of(x)]
        send(("x", u, ch, 1), own, own, at(dx=1))
        send(("x", u, ch, 3), own, own, at(dx=3))
        send(("c", u, ch, 0), own, own, at(dc=1))

    def side_on(u):
        half = TR // 2
        got(("y", u, 1))
        src = a.at[u, pl.ds(0, half), lanes(lax.rem(y + 3, 4))]
        send(("yy", u, 1), src, src, at(dy=1))
        got(("y", u, 3))
        src = a.at[u, pl.ds(half, half), lanes(lax.rem(y + 1, 4))]
        send(("yy", u, 3), src, src, at(dy=3))

    def spread_on(u, ch):
        before, after = lax.rem(x + 3, 4), lax.rem(x + 1, 4)
        got(("x", u, ch, 1))
        src = b.at[u, ch, rows_of(before, 0, SUB // 2)]
        send(("xx", u, ch, 1), src, src, at(dx=1))
        src = b.at[u, ch, rows_of(before)]
        send(("c", u, ch, 1), src, src, at(dc=1))
        got(("x", u, ch, 3))
        src = b.at[u, ch, rows_of(after, SUB // 2, SUB // 2)]
        send(("xx", u, ch, 3), src, src, at(dx=3))
        src = b.at[u, ch, rows_of(after)]
        send(("c", u, ch, 3), src, src, at(dc=1))

    def spread_last(u, ch):
        across = lax.rem(x + 2, 4)
        got(("xx", u, ch, 1))
        src = b.at[u, ch, rows_of(across, 0, SUB // 2)]
        send(("c", u, ch, 2), src, src, at(dc=1))
        got(("xx", u, ch, 3))
        src = b.at[u, ch, rows_of(across, SUB // 2, SUB // 2)]
        send(("c", u, ch, 4), src, src, at(dc=1))

    def side_ready(u):
        got(("yy", u, 1), ("yy", u, 3))

    def chunk_ready(u, ch):
        got(*(("c", u, ch, i) for i in range(5)))

    def multiply(p, left, right, ch, add=False):
        @pl.loop(0, 3)
        def _(n):
            cols = pl.ds(pl.multiple_of(n * 256, 256), 256)
            value = jnp.dot(a[left], b[right, ch, :, cols], preferred_element_type=F32)
            if add:
                total[p, ch, :, cols] += value
            else:
                total[p, ch, :, cols] = value

    half = TR // 2

    def sum_far(r, p):
        part[r, 1] = total[p, 0, :, 0:TC].astype(BF)
        send(("s2", r, 1), part.at[r, 1, pl.ds(0, half)], far.at[r, 0], at(dz=1))
        send(("s2", r, 3), part.at[r, 1, pl.ds(half, half)], far.at[r, 1], at(dz=3))

    def sum_up(r, p):
        got(("s2", r, 1))
        part[r, 0, 0:half] = (total[p, 0, 0:half, TC:] + far[r, 0].astype(F32)).astype(BF)
        part[r, 0, half:] = total[p, 0, half:, TC:].astype(BF)
        send(("s1", r, 1), part.at[r, 0], near.at[r, 0], at(dz=1))

    def sum_down(r, p):
        got(("s2", r, 3))
        part[r, 2, 0:half] = total[p, 1, 0:half, 0:TC].astype(BF)
        part[r, 2, half:] = (total[p, 1, half:, 0:TC] + far[r, 1].astype(F32)).astype(BF)
        send(("s1", r, 3), part.at[r, 2], near.at[r, 1], at(dz=3))

    inv_root = 1.0 / math.sqrt(6144)

    def finish(r, p, which, old, write):
        got(("s1", r, 1), ("s1", r, 3))

        @pl.loop(0, TR // BLK)
        def _(i):
            rows = pl.ds(pl.multiple_of(i * BLK, BLK), BLK)
            for j in range(TC // BLK):
                cs = slice(j * BLK, (j + 1) * BLK)
                big_row, big_col = row * (TR // BLK) + i, col * (TC // BLK) + j
                keep = jnp.where(big_row == big_col, 1, patterns[which, big_row, big_col]).astype(F32)
                value = (
                    total[p, 1, rows, TC + j * BLK : TC + (j + 1) * BLK]
                    + near[r, 0, rows, cs].astype(F32)
                    + near[r, 1, rows, cs].astype(F32)
                ) * inv_root
                if old is not None:
                    mine = pl.ds(pl.multiple_of(y * TC + j * BLK, BLK), BLK)
                    value = 2.0 * a[old, rows, mine].astype(F32) - value
                write(rows, j, keep * value)

    def to_unit(u):
        def write(rows, j, value):
            a[u, rows, pl.ds(pl.multiple_of(y * TC + j * BLK, BLK), BLK)] = value.astype(BF)
        return write

    def to_out(ref):
        def write(rows, j, value):
            ref[rows, j * BLK : (j + 1) * BLK] = value
        return write

    move("zero", zero_hbm, tile(0))
    move("first", first_hbm, tile(1))
    barrier = pltpu.get_barrier_semaphore()
    for peer in peers:
        pl.semaphore_signal(barrier, inc=1, device_id=peer, device_id_type=MESH)
    pl.semaphore_wait(barrier, len(peers))

    locals_["zero"].wait()
    begin_turn(0)
    begin_side(0)
    turn_z(0)
    spread_own(0, 0)
    spread_own(0, 1)
    locals_["first"].wait()
    begin_turn(1)
    side_on(0)
    begin_side(1)
    spread_on(0, 0)
    spread_on(0, 1)
    turn_z(1)
    spread_last(0, 0)
    spread_last(0, 1)
    spread_own(1, 0)
    spread_own(1, 1)
    side_ready(0)
    chunk_ready(0, 0)
    multiply(0, 0, 0, 0)
    sum_far(0, 0)
    chunk_ready(0, 1)
    multiply(0, 0, 0, 1)
    side_on(1)
    sum_up(0, 0)
    sum_down(0, 0)
    side_ready(1)
    spread_on(1, 0)
    spread_on(1, 1)
    multiply(1, 1, 0, 0)
    multiply(1, 1, 0, 1)
    spread_last(1, 0)
    spread_last(1, 1)
    finish(0, 0, 0, None, to_unit(2))
    begin_turn(2)
    begin_side(2)
    chunk_ready(1, 0)
    multiply(1, 0, 1, 0, add=True)
    sum_far(1, 1)
    chunk_ready(1, 1)
    multiply(1, 0, 1, 1, add=True)
    turn_z(2)
    sum_up(1, 1)
    sum_down(1, 1)
    side_on(2)
    spread_own(2, 0)
    spread_own(2, 1)
    finish(1, 1, 1, None, to_unit(3))
    begin_turn(3)
    begin_side(3)
    spread_on(2, 0)
    spread_on(2, 1)
    spread_last(2, 0)
    spread_last(2, 1)
    turn_z(3)
    spread_own(3, 0)
    spread_own(3, 1)
    side_ready(2)
    chunk_ready(2, 0)
    multiply(0, 2, 2, 0)
    sum_far(2, 0)
    chunk_ready(2, 1)
    multiply(0, 2, 2, 1)
    side_on(3)
    sum_up(2, 0)
    sum_down(2, 0)
    side_ready(3)
    spread_on(3, 0)
    spread_on(3, 1)
    multiply(1, 3, 2, 0)
    multiply(1, 3, 2, 1)
    spread_last(3, 0)
    spread_last(3, 1)
    chunk_ready(3, 0)
    multiply(1, 2, 3, 0, add=True)
    sum_far(3, 1)
    chunk_ready(3, 1)
    multiply(1, 2, 3, 1, add=True)
    sum_up(3, 1)
    sum_down(3, 1)
    finish(2, 0, 0, 2, to_out(out_zero))
    finish(3, 1, 1, 3, to_out(out_first))
    for copy in copies.values():
        copy.wait_send()


def on_device(density, strips, dest_device, atom_slot, block_slot, patterns):
    linear = start_linear(strips, dest_device, atom_slot, block_slot, patterns)
    out = jax.ShapeDtypeStruct((TR, TC), F32)
    return tuple(pl.pallas_call(
        kernel,
        out_shape=(out, out),
        in_specs=[
            pl.BlockSpec(memory_space=pl.ANY),
            pl.BlockSpec(memory_space=pl.ANY),
            pl.BlockSpec(memory_space=pltpu.SMEM),
        ],
        out_specs=(pl.BlockSpec(memory_space=pltpu.VMEM),) * 2,
        scratch_shapes=[
            pltpu.VMEM((4, TR, KB), BF),
            pltpu.VMEM((4, 2, KB, 2 * TC), BF),
            pltpu.VMEM((4, 4, SUB, TC), BF),
            pltpu.VMEM((2, 2, TR, 2 * TC), F32),
            pltpu.VMEM((4, 3, TR, TC), BF),
            pltpu.VMEM((4, 2, TR, TC), BF),
            pltpu.VMEM((4, 2, TR // 2, TC), BF),
            pltpu.SemaphoreType.DMA((N_COPIES,)),
            pltpu.SemaphoreType.DMA((N_COPIES,)),
            pltpu.SemaphoreType.DMA((16,)),
        ],
        compiler_params=pltpu.CompilerParams(
            collective_id=0, has_side_effects=True, vmem_limit_bytes=62 * 2**20 - 2**19
        ),
        cost_estimate=pl.CostEstimate(flops=21743271936, bytes_accessed=8 * 2**20, transcendentals=0),
    )(density, linear, patterns))


def solution(mesh):
    return jax.shard_map(
        on_device,
        mesh=mesh,
        in_specs=(
            P("row", "col"),
            P(("row", "col"), None, None),
            P(("row", "col"), None),
            P(("row", "col")),
            P(("row", "col")),
            P(),
        ),
        out_specs=(P("row", "col"), P("row", "col")),
        check_vma=False,
    )
```

time: 541 us -> 213 us (0.39)
  waiting for transfers between devices: 415 us -> 13.9 us
  Pallas kernels: 0 us -> 175 us
  matrix products: 58.5 us -> 0.78 us
  local copies, waits for them, and re-layouts: 22.8 us -> 6.66 us
  starting transfers between devices: 26.2 us -> 11.5 us
  between operations: 14.4 us -> 0.76 us
    all_gather x8 -> x0, waiting for transfers between devices: 392 us -> none  [the longest x2 170 us: products(): lax.all_gather(zeroth, 'col', axis=1, tiled=True)]
    pallas_call x0 -> x1, Pallas kernels: none -> 175 us  [on_device(): pl.pallas_call(kernel, out_shape=(out, out), in_specs=[pl.BlockSpec(memor...]
    dot_general x7 -> x2, matrix products: 58.5 us -> 0.78 us  [the longest x1 0.48 us: start_linear(): lax.dot_general(placing.astype(BF), got[:, :atom_width * width], (((0,),...]
    scatter x3 -> x0, local copies, waits for them, and re-layouts: 15.6 us -> none  [the longest x1 13.4 us: on_device(): sent_strips = jnp.zeros((devices * capacity, atom_width, block_width), st...]
    all_to_all x3 -> x1, starting transfers between devices: 25.7 us -> 11.5 us  [start_linear(): lax.all_to_all(sent.reshape(devices, CAPACITY, (atom_width + 1) * width),...]
    all_to_all x3 -> x1, waiting for transfers between devices: 19.2 us -> 13.9 us  [start_linear(): lax.all_to_all(sent.reshape(devices, CAPACITY, (atom_width + 1) * width),...]
  transfers between devices with their start and end apart: 11 -> 1, of which waited for: 9 -> 1; matrix products, arithmetic and copies ran while one was open for 12% -> 0% of each run, Pallas kernels for 0% -> 0%
where the time goes in v2:
time: 213 us
  Pallas kernels  175 us (82%)
  waiting for transfers between devices  13.9 us (7%)
  starting transfers between devices  11.5 us (5%)
  local copies, waits for them, and re-layouts  6.66 us (3%)
  other arithmetic  4.31 us (2%)
    pallas_call x1, Pallas kernels, on_device(): pl.pallas_call(kernel, out_shape=(out, out), in_specs=[pl.BlockSpec(memor...  175 us
    all_to_all x1, waiting for transfers between devices, start_linear(): lax.all_to_all(sent.reshape(devices, CAPACITY, (atom_width + 1) * width),...  13.9 us
    all_to_all x1, starting transfers between devices, start_linear(): lax.all_to_all(sent.reshape(devices, CAPACITY, (atom_width + 1) * width),...  11.5 us
    unnamed x8, local copies, waits for them, and re-layouts  4.78 us
  transfers between devices with their start and end apart: 1, of which 1 were waited for; matrix products, arithmetic and copies ran while one was open for 0% of the time, Pallas kernels for 0%

profile of v2, /device:TPU:1, one launch (start us, length us, event | category | flops | bytes accessed | tf_op | source)
XLA Modules:
  0.0 212.7 jit_solution(18128496086974928181)
XLA Ops:
  0.6 0.7 broadcast_add_fusion
  1.3 0.9 convert_reduce_fusion
  2.2 0.7 multiply_add_fusion
  2.9 1.0 copy.22
  3.9 0.8 select_convert_fusion
  4.6 0.3 convolution_convert_fusion
  4.9 0.0 slice-start
  5.0 1.0 reshape.60
  6.0 11.5 %all-to-all-start = ((bf16[128,2,1152]{2,1,0:T(2,128)(2,1)}), bf16[128,2,1152]{2,1,0:T(2,128)(2,1)S(1)}, u32[]{:S(2)}, u32[]{:S(2)}) async-start(bf16[128,2,1152]{2,1,0:T(2,128)(2,1)} %reshape.60), calls=%async_computation | async-start | bytes 1179648 | tf_op jit(solution)/shard_map/all_to_all | solution.py:51
  17.5 0.0 slice-done
  17.5 0.1 constant_dynamic-slice_fusion
  17.6 0.1 copy.15
  17.7 0.1 fusion.14
  17.8 0.1 broadcast_bitcast_fusion
  17.9 0.1 broadcast_in_dim.55
  17.9 0.4 copy.16
  18.3 13.9 %all-to-all-done = bf16[128,2,1152]{2,1,0:T(2,128)(2,1)S(1)} async-done(((bf16[128,2,1152]{2,1,0:T(2,128)(2,1)}), bf16[128,2,1152]{2,1,0:T(2,128)(2,1)S(1)}, u32[]{:S(2)}, u32[]{:S(2)}) %all-to-all-start) | async-done | bytes 589856 | tf_op jit(solution)/shard_map/all_to_all | solution.py:51
  32.2 0.2 reshape.61
  32.5 0.1 fusion.11
  32.6 0.2 add_reduce_fusion
  32.8 0.5 convolution_bitcast_fusion
  33.2 0.2 copy.19
  33.5 0.9 fusion.1.first_hbm
  34.4 174.7 %shard_map.77 = (f32[768,384]{1,0:T(8,128)}, f32[768,384]{1,0:T(8,128)}) custom-call(bf16[768,384]{1,0:T(8,128)(2,1)} %zero_hbm.1, bf16[768,384]{1,0:T(8,128)(2,1)} %fusion.1.first_hbm, s32[3,48,48]{2,1,0:T(8,128)} %patterns.1), custom_call_target="tpu_custom_call" | custom-call | flops 21743271936 | bytes 8388608 | tf_op jit(solution)/shard_map/pallas_call | solution.py:346
  209.2 0.0 copy-start
  209.2 2.5 %copy.26 = f32[768,384]{1,0:T(8,128)} copy(f32[768,384]{1,0:T(8,128)} %get-tuple-element.6) | data formatting | bytes 2359296
  211.7 0.0 copy-done
  211.7 1.0 copy.27
  (4 shorter events, 0.0 us)
Async XLA Ops:
  4.9 12.6 %slice-start = ((s32[3,48,48]{2,1,0:T(8,128)}), s32[1,48,48]{2,1,0:T(8,128)S(1)}, s32[]{:S(2)}) async-start(s32[3,48,48]{2,1,0:T(8,128)} %patterns.1), calls=%async_computation.1 | async-start | bytes 49152 | tf_op jit(solution)/shard_map/slice | solution.py:24
  6.0 26.2 %all-to-all-start = ((bf16[128,2,1152]{2,1,0:T(2,128)(2,1)}), bf16[128,2,1152]{2,1,0:T(2,128)(2,1)S(1)}, u32[]{:S(2)}, u32[]{:S(2)}) async-start(bf16[128,2,1152]{2,1,0:T(2,128)(2,1)} %reshape.60), calls=%async_computation | async-start | bytes 1179648 | tf_op jit(solution)/shard_map/all_to_all | solution.py:51
  209.2 2.5 %copy-start = (f32[768,384]{1,0:T(8,128)S(1)}, f32[768,384]{1,0:T(8,128)}, u32[]{:S(2)}) copy-start(f32[768,384]{1,0:T(8,128)} %get-tuple-element.7) | copy-start | bytes 3538948

commit v3 on v1

v3 whole, which is shorter than its diff:
```python
import math

import jax
import jax.numpy as jnp
from jax import lax
from jax.experimental import pallas as pl
from jax.experimental.pallas import tpu as pltpu
from jax.sharding import PartitionSpec as P

MESH = pl.DeviceIdType.MESH
BF = jnp.bfloat16
F32 = jnp.float32
I32 = jnp.int32
TR, TC = 768, 384
HALF = TR // 2
KB = 1536
SUB = TR // 4
BLK = 128
ATOM = 8
ITEMS = 128
SLOTS = 256
WIDE = ATOM * BLK + BLK
ATOMS = TR // ATOM
N_COPIES = 224


def kernel(
    zero_hbm, strips, dest, atoms, blocks, patterns, out_zero, out_first,
    a, b, turn, total, part, near, far, rows, sent, came, placed, send_sem, recv_sem, local_sem,
):
    row, col = lax.axis_index("row"), lax.axis_index("col")
    x, core = row // 2, row % 2
    z, y = col // 4, col % 4

    def at(dx=0, dz=0, dy=0, dc=0):
        nx, nz, ny = (lax.rem(x + dx, 4), lax.rem(z + dz, 4), lax.rem(y + dy, 4))
        return {"row": nx * 2 + lax.rem(core + dc, 2), "col": nz * 4 + ny}

    copies, moves = {}, {}
    arrived, left = set(), set()

    def send(name, src, dst, device):
        i = len(copies)
        copies[name] = pltpu.make_async_remote_copy(
            src_ref=src, dst_ref=dst, send_sem=send_sem.at[i], recv_sem=recv_sem.at[i],
            device_id=device, device_id_type=MESH,
        )
        copies[name].start()

    def move(name, src, dst):
        moves[name] = pltpu.make_async_copy(src, dst, local_sem.at[len(moves)])
        moves[name].start()

    def got(*names):
        for name in names:
            if name not in arrived:
                arrived.add(name)
                if name in copies:
                    copies[name].wait_recv()
                else:
                    moves[name].wait()

    def gone(*names):
        for name in names:
            if name not in left:
                left.add(name)
                copies[name].wait_send()

    def lanes(position):
        return pl.ds(pl.multiple_of(position * TC, BLK), TC)

    def rows_of(position, first=0, size=SUB):
        return pl.ds(pl.multiple_of(core * TR + position * SUB + first, 32), size)

    def rows_at(position, size):
        return pl.ds(pl.multiple_of(position * size, 32), size)

    def tile(u, where=slice(None)):
        return a.at[u, where, lanes(y)]

    def begin_turn(u):
        if u == 0:
            got("zero")
        for dx in (2, 1, 3):
            src = tile(u, rows_at(lax.rem(x + dx, 4), SUB))
            send(("tx", u, dx), src, turn.at[u, 4 - dx], at(dx=dx))
        move(("t0", u), tile(u, rows_at(x, SUB)), turn.at[u, 0])

    def turn_z(u):
        got(("tx", u, 2), ("tx", u, 1), ("tx", u, 3), ("t0", u))
        for dz in (2, 3, 1, 0):
            src = turn.at[u, lax.rem(z + dz + 4 - x, 4)]
            dst = b.at[u, (4 - dz) % 4, rows_of(x)]
            if dz:
                send(("tz", u, 4 - dz), src, dst, at(dz=dz))
            else:
                move(("tz", u, 0), src, dst)

    def own(u, k):
        got(("tz", u, k))
        src = b.at[u, k, rows_of(x)]
        send(("x", u, k, 1), src, src, at(dx=1))
        send(("x", u, k, 3), src, src, at(dx=3))
        send(("c", u, k, 0), src, src, at(dc=1))

    def fwd(u, k, h):
        got(("x", u, k, h))
        source = lax.rem(x + 4 - h, 4)
        src = b.at[u, k, rows_of(source, SUB // 2 if h == 3 else 0, SUB // 2)]
        send(("xx", u, k, h), src, src, at(dx=h))
        src = b.at[u, k, rows_of(source)]
        send(("c", u, k, h), src, src, at(dc=1))

    def last(u, k, h):
        got(("xx", u, k, h))
        src = b.at[u, k, rows_of(lax.rem(x + 2, 4), SUB // 2 if h == 3 else 0, SUB // 2)]
        send(("c", u, k, h + 1), src, src, at(dc=1))

    def begin_side(u):
        send(("y", u, 1), tile(u), tile(u), at(dy=1))
        send(("y", u, 3), tile(u), tile(u), at(dy=3))

    def side_on(u, h):
        got(("y", u, h))
        where = pl.ds(HALF if h == 3 else 0, HALF)
        src = a.at[u, where, lanes(lax.rem(y + 4 - h, 4))]
        send(("yy", u, h), src, src, at(dy=h))

    def product(left_unit, right_unit, k):
        got(("y", left_unit, 1), ("y", left_unit, 3), ("yy", left_unit, 1), ("yy", left_unit, 3))
        got(("tz", right_unit, k), *(("c", right_unit, k, i) for i in range(5)))
        for h in (1, 3):
            got(("x", right_unit, k, h), ("xx", right_unit, k, h))
        return jnp.dot(a[left_unit], b[right_unit, k], preferred_element_type=F32)

    def sq(s, k):
        total[0, k] = product(2 * s, 2 * s, k)

    def cra(s, k):
        total[1, k] = product(2 * s + 1, 2 * s, k)

    def crb(s, k):
        total[1, k] += product(2 * s, 2 * s + 1, k)

    def far_names(r):
        return [(kind, r, h) for kind in ("s2", "sf", "sd") for h in (1, 3)]

    def send_far(r):
        p = r % 2
        if r > 1:
            gone(*far_names(r - 2))
        part[p, 1] = total[p, 2].astype(BF)
        send(("s2", r, 1), part.at[p, 1, pl.ds(0, HALF)], far.at[r, 0], at(dz=1))
        send(("s2", r, 3), part.at[p, 1, pl.ds(HALF, HALF)], far.at[r, 1], at(dz=3))

    def free(r, h):
        p, i, k = r % 2, h // 2, h
        where = pl.ds(HALF if h == 1 else 0, HALF)
        part[p, 2 * i, where] = total[p, k, where].astype(BF)
        send(("sf", r, h), part.at[p, 2 * i, where], near.at[r, i, where], at(dz=h))

    def dep(r, h):
        p, i, k = r % 2, h // 2, h
        where = pl.ds(0 if h == 1 else HALF, HALF)
        got(("s2", r, h))
        part[p, 2 * i, where] = (total[p, k, where] + far[r, i].astype(F32)).astype(BF)
        send(("sd", r, h), part.at[p, 2 * i, where], near.at[r, i, where], at(dz=h))

    def keep(which, i, j):
        big_row, big_col = row * (TR // BLK) + i, col * (TC // BLK) + j
        return jnp.where(big_row == big_col, 1, patterns[which, big_row, big_col]).astype(F32)

    inv_root = 1.0 / math.sqrt(6144)

    def finish(r):
        p = r % 2
        got(("sf", r, 1), ("sf", r, 3), ("sd", r, 1), ("sd", r, 3))

        @pl.loop(0, TR // BLK)
        def _(i):
            where = pl.ds(pl.multiple_of(i * BLK, BLK), BLK)
            for j in range(TC // BLK):
                cs = slice(j * BLK, (j + 1) * BLK)
                mine = pl.ds(pl.multiple_of(y * TC + j * BLK, BLK), BLK)
                value = (
                    total[p, 0, where, cs]
                    + near[r, 0, where, cs].astype(F32)
                    + near[r, 1, where, cs].astype(F32)
                ) * inv_root
                if r < 2:
                    a[r + 2, where, mine] = (keep(p, i, j) * value).astype(BF)
                else:
                    value = 2.0 * a[r, where, mine].astype(F32) - value
                    out = (out_zero, out_first)[p]
                    out[where, cs] = keep(p, i, j) * value

    def iota(shape, dim):
        return lax.broadcasted_iota(I32, shape, dim)

    def ones(condition):
        return jnp.where(condition, 1.0, 0.0).astype(BF)

    def strips_place():
        named = jnp.broadcast_to(dest[...].astype(F32), (ITEMS, ITEMS))
        square = (ITEMS, ITEMS)
        earlier = (named == named.T) & (iota(square, 1) < iota(square, 0))
        rank = jnp.sum(jnp.where(earlier, 1.0, 0.0), axis=1, keepdims=True).astype(I32)
        d = dest[...]
        place = (d & 3) * 64 + (d >> 4) * 8 + ((d >> 2) & 3) * 2 + rank
        atom = jnp.broadcast_to(atoms[...].astype(F32), square).T
        block = jnp.broadcast_to(blocks[...].astype(F32), square).T
        lane = iota(square, 1)
        tags = jnp.where(lane == 0, atom + 1.0, jnp.where(lane == 1, block, 0.0))
        rows[:, : ATOM * BLK] = strips[...]
        rows[:, ATOM * BLK :] = tags.astype(BF)
        spread = ones(iota((ITEMS, SLOTS), 1) == place)
        sent[0] = lax.dot_general(
            spread, rows[...], (((0,), (0,)), ((), ())), preferred_element_type=F32
        ).astype(BF)

    def reorder(i, source):
        taken = ones(iota((SLOTS, SLOTS), 1) == source(iota((SLOTS, SLOTS), 0)))
        sent[i] = jnp.dot(taken, came[i - 1], preferred_element_type=F32).astype(BF)

    def strips_y():
        src = rows_at(y, 64)
        for dy in (2, 1, 3):
            send(("gy", dy), sent.at[0, rows_at(lax.rem(y + dy, 4), 64)], came.at[0, src], at(dy=dy))
        move(("gy", 0), sent.at[0, src], came.at[0, src])

    def strips_x():
        got(("gy", 0), ("gy", 1), ("gy", 2), ("gy", 3))
        reorder(1, lambda o: ((o >> 1) & 3) * 64 + (o >> 5) * 8 + ((o >> 3) & 3) * 2 + (o & 1))
        mine = rows_at(row, 32)
        for dx in (2, 1, 3, 0):
            for dc in (0, 1):
                if dx or dc:
                    target = lax.rem(x + dx, 4) * 2 + lax.rem(core + dc, 2)
                    src = sent.at[1, rows_at(target, 32)]
                    send(("gx", dx, dc), src, came.at[1, mine], at(dx=dx, dc=dc))
        move(("gx", 0, 0), sent.at[1, mine], came.at[1, mine])

    def strips_z():
        got(*(("gx", dx, dc) for dx in range(4) for dc in range(2)))
        reorder(2, lambda o: ((o >> 3) & 7) * 32 + (o >> 6) * 8 + (o & 7))
        mine = rows_at(z, 64)
        for dz in (2, 1, 3):
            send(("gz", dz), sent.at[2, rows_at(lax.rem(z + dz, 4), 64)], came.at[2, mine], at(dz=dz))
        move(("gz", 0), sent.at[2, mine], came.at[2, mine])

    def field():
        got(("gz", 0), ("gz", 1), ("gz", 2), ("gz", 3))
        tags = came[2, :, ATOM * BLK :].astype(F32)
        atom, block = tags[:, 0:1], tags[:, 1:2]
        cell = jnp.where(atom > 0.0, block * ATOMS + atom - 1.0, -1.0)
        placing = ones(iota((SLOTS, TC), 1).astype(F32) == cell)
        summed = lax.dot_general(
            placing, came[2, :, : ATOM * BLK], (((0,), (0,)), ((), ())), preferred_element_type=F32
        )
        for j in range(TC // BLK):
            for i in range(ATOM):
                placed[j, pl.ds(i, ATOMS, stride=ATOM), :] = summed[
                    j * ATOMS : (j + 1) * ATOMS, i * BLK : (i + 1) * BLK
                ]

        @pl.loop(0, TR // BLK)
        def _(i):
            where = pl.ds(pl.multiple_of(i * BLK, BLK), BLK)
            for j in range(TC // BLK):
                mine = pl.ds(pl.multiple_of(y * TC + j * BLK, BLK), BLK)
                value = keep(2, i, j) * placed[j, where, :]
                a[1, where, mine] = (-value).astype(BF)

    move("zero", zero_hbm, tile(0))
    peers = [at(dx=dx, dc=dc) for dx in range(4) for dc in range(2) if dx or dc]
    peers += [at(dz=d) for d in (1, 2, 3)] + [at(dy=d) for d in (1, 2, 3)]
    barrier = pltpu.get_barrier_semaphore()
    for peer in peers:
        pl.semaphore_signal(barrier, inc=1, device_id=peer, device_id_type=MESH)
    strips_place()
    pl.semaphore_wait(barrier, len(peers))

    strips_y()
    begin_turn(0)
    begin_side(0)
    strips_x()
    turn_z(0)
    own(0, 2)
    strips_z()
    fwd(0, 2, 3)
    fwd(0, 2, 1)
    side_on(0, 1)
    own(0, 1)
    own(0, 3)
    side_on(0, 3)
    last(0, 2, 3)
    last(0, 2, 1)
    field()
    begin_turn(1)
    begin_side(1)
    fwd(0, 1, 3)
    fwd(0, 1, 1)
    own(0, 0)
    sq(0, 2)
    send_far(0)
    fwd(0, 3, 1)
    fwd(0, 3, 3)
    turn_z(1)
    last(0, 1, 3)
    last(0, 1, 1)
    sq(0, 1)
    free(0, 1)
    fwd(0, 0, 3)
    dep(0, 1)
    fwd(0, 0, 1)
    own(1, 2)
    last(0, 3, 3)
    side_on(1, 3)
    last(0, 3, 1)
    side_on(1, 1)
    last(0, 0, 3)
    last(0, 0, 1)
    sq(0, 3)
    free(0, 3)
    own(1, 1)
    dep(0, 3)
    sq(0, 0)
    fwd(1, 2, 1)
    fwd(1, 2, 3)
    own(1, 3)
    cra(0, 2)
    fwd(1, 1, 1)
    fwd(1, 1, 3)
    own(1, 0)
    last(1, 2, 3)
    last(1, 2, 1)
    cra(0, 1)
    cra(0, 0)
    crb(0, 2)
    fwd(1, 3, 1)
    send_far(1)
    last(1, 1, 1)
    fwd(1, 3, 3)
    last(1, 1, 3)
    cra(0, 3)
    crb(0, 1)
    finish(0)
    begin_turn(2)
    begin_side(2)
    last(1, 3, 3)
    fwd(1, 0, 3)
    last(1, 3, 1)
    fwd(1, 0, 1)
    free(1, 1)
    dep(1, 1)
    crb(0, 3)
    free(1, 3)
    turn_z(2)
    last(1, 0, 1)
    last(1, 0, 3)
    crb(0, 0)
    dep(1, 3)
    side_on(2, 3)
    side_on(2, 1)
    own(2, 2)
    own(2, 1)
    fwd(2, 2, 3)
    fwd(2, 2, 1)
    own(2, 3)
    finish(1)
    begin_turn(3)
    fwd(2, 1, 1)
    begin_side(3)
    fwd(2, 1, 3)
    last(2, 2, 3)
    last(2, 2, 1)
    sq(1, 2)
    send_far(2)
    fwd(2, 3, 3)
    fwd(2, 3, 1)
    turn_z(3)
    last(2, 1, 1)
    last(2, 1, 3)
    last(2, 3, 3)
    last(2, 3, 1)
    side_on(3, 1)
    side_on(3, 3)
    sq(1, 1)
    own(3, 2)
    free(2, 1)
    dep(2, 1)
    sq(1, 3)
    free(2, 3)
    dep(2, 3)
    own(3, 1)
    fwd(3, 2, 3)
    fwd(3, 2, 1)
    own(3, 3)
    cra(1, 2)
    fwd(3, 1, 1)
    fwd(3, 1, 3)
    cra(1, 1)
    last(3, 2, 1)
    last(3, 2, 3)
    cra(1, 3)
    crb(1, 2)
    send_far(3)
    fwd(3, 3, 1)
    fwd(3, 3, 3)
    own(3, 0)
    last(3, 1, 1)
    last(3, 1, 3)
    last(3, 3, 1)
    last(3, 3, 3)
    crb(1, 1)
    free(3, 1)
    crb(1, 3)
    free(3, 3)
    fwd(3, 0, 3)
    fwd(3, 0, 1)
    dep(3, 1)
    last(3, 0, 3)
    last(3, 0, 1)
    own(2, 0)
    dep(3, 3)
    fwd(2, 0, 3)
    fwd(2, 0, 1)
    last(2, 0, 3)
    last(2, 0, 1)
    cra(1, 0)
    crb(1, 0)
    sq(1, 0)
    finish(2)
    finish(3)

    got(*copies, *moves)
    gone(*copies)


def on_device(density, strips, dest_device, atom_slot, block_slot, patterns):
    out = jax.ShapeDtypeStruct((TR, TC), F32)
    vmem = pl.BlockSpec(memory_space=pltpu.VMEM)
    return tuple(pl.pallas_call(
        kernel,
        out_shape=(out, out),
        in_specs=[
            pl.BlockSpec(memory_space=pl.ANY), vmem, vmem, vmem, vmem,
            pl.BlockSpec(memory_space=pltpu.SMEM),
        ],
        out_specs=(vmem, vmem),
        scratch_shapes=[
            pltpu.VMEM((4, TR, KB), BF),
            pltpu.VMEM((4, 4, KB, TC), BF),
            pltpu.VMEM((4, 4, SUB, TC), BF),
            pltpu.VMEM((2, 4, TR, TC), F32),
            pltpu.VMEM((2, 3, TR, TC), BF),
            pltpu.VMEM((4, 2, TR, TC), BF),
            pltpu.VMEM((4, 2, HALF, TC), BF),
            pltpu.VMEM((ITEMS, WIDE), BF),
            pltpu.VMEM((3, SLOTS, WIDE), BF),
            pltpu.VMEM((3, SLOTS, WIDE), BF),
            pltpu.VMEM((TC // BLK, TR, BLK), F32),
            pltpu.SemaphoreType.DMA((N_COPIES,)),
            pltpu.SemaphoreType.DMA((N_COPIES,)),
            pltpu.SemaphoreType.DMA((16,)),
        ],
        compiler_params=pltpu.CompilerParams(
            collective_id=0, has_side_effects=True, vmem_limit_bytes=62 * 2**20 - 2**19
        ),
        cost_estimate=pl.CostEstimate(flops=21743271936, bytes_accessed=8 * 2**20, transcendentals=0),
    )(
        density,
        strips.reshape(ITEMS, ATOM * BLK),
        dest_device,
        atom_slot.reshape(1, ITEMS),
        block_slot.reshape(1, ITEMS),
        patterns,
    ))


def solution(mesh):
    return jax.shard_map(
        on_device,
        mesh=mesh,
        in_specs=(
            P("row", "col"),
            P(("row", "col"), None, None),
            P(("row", "col"), None),
            P(("row", "col")),
            P(("row", "col")),
            P(),
        ),
        out_specs=(P("row", "col"), P("row", "col")),
        check_vma=False,
    )
```

time: 541 us -> 175 us (0.32)
  waiting for transfers between devices: 415 us -> 0 us
  Pallas kernels: 0 us -> 167 us
  matrix products: 58.5 us -> 0 us
  starting transfers between devices: 26.2 us -> 0 us
  local copies, waits for them, and re-layouts: 22.8 us -> 6.56 us
  between operations: 14.4 us -> 0.65 us
    all_gather x8 -> x0, waiting for transfers between devices: 392 us -> none  [the longest x2 170 us: products(): lax.all_gather(zeroth, 'col', axis=1, tiled=True)]
    pallas_call x0 -> x1, Pallas kernels: none -> 167 us  [on_device(): pl.pallas_call(kernel, out_shape=(out, out), in_specs=[pl.BlockSpec(memor...]
    dot_general x7 -> x0, matrix products: 58.5 us -> none  [the longest x2 19.6 us: products(): jnp.dot(pieces[0], col_first, preferred_element_type=jnp.float32)]
    all_to_all x3 -> x0, starting transfers between devices: 25.7 us -> none  [the longest x1 11.5 us: on_device(): lax.all_to_all(sent_blocks.reshape(devices, capacity), ('row', 'col'), sp...]
    all_to_all x3 -> x0, waiting for transfers between devices: 19.2 us -> none  [the longest x1 12.7 us: on_device(): lax.all_to_all(sent_strips.reshape(devices, capacity, atom_width, block_w...]
    scatter x3 -> x0, local copies, waits for them, and re-layouts: 15.6 us -> none  [the longest x1 13.4 us: on_device(): sent_strips = jnp.zeros((devices * capacity, atom_width, block_width), st...]
    unnamed x13 -> x6, local copies, waits for them, and re-layouts: 0.34 us -> 6.56 us
  transfers between devices with their start and end apart: 11 -> 0, of which waited for: 9 -> 0; matrix products, arithmetic and copies ran while one was open for 12% -> 0% of each run, Pallas kernels for 0% -> 0%
where the time goes in v3:
time: 175 us; the launch traced here: 174 us
  Pallas kernels  167 us (95%)
  local copies, waits for them, and re-layouts  6.56 us (4%)
    pallas_call x1, Pallas kernels, on_device(): pl.pallas_call(kernel, out_shape=(out, out), in_specs=[pl.BlockSpec(memor...  167 us
    unnamed x6, local copies, waits for them, and re-layouts  6.56 us

profile of v3, /device:TPU:1, one launch (start us, length us, event | category | flops | bytes accessed | tf_op | source)
XLA Modules:
  0.0 174.5 jit_solution(2562118893003817838)
XLA Ops:
  0.6 1.4 copy.8.dest
  2.0 1.7 copy.11
  3.7 167.3 %shard_map.77 = (f32[768,384]{1,0:T(8,128)}, f32[768,384]{1,0:T(8,128)}) custom-call(bf16[768,384]{1,0:T(8,128)(2,1)} %zero_hbm.1, bf16[128,1024]{1,0:T(8,128)(2,1)} %bitcast.7, s32[128,1]{1,0:T(8,128)} %copy.8.dest, s32[1,128]{1,0:T(1,128)} %bitcast.8, s32[1,128]{1,0:T(1,128)} %bitcast.9, s32[3,48,48]{2,1,0:T(8,128)} %patterns.1), custom_call_target="tpu_custom_call" | custom-call | flops 21743271936 | bytes 8388608 | tf_op jit(solution)/shard_map/pallas_call | solution.py:443
  171.0 0.0 copy-start
  171.0 2.5 %copy.14 = f32[768,384]{1,0:T(8,128)} copy(f32[768,384]{1,0:T(8,128)} %get-tuple-element.4) | data formatting | bytes 2359296
  173.5 0.0 copy-done
  173.5 1.0 copy.15
Async XLA Ops:
  171.0 2.5 %copy-start = (f32[768,384]{1,0:T(8,128)S(1)}, f32[768,384]{1,0:T(8,128)}, u32[]{:S(2)}) copy-start(f32[768,384]{1,0:T(8,128)} %get-tuple-element.5) | copy-start | bytes 3538948

commit v4 on v3

v4 whole, which is shorter than its diff:
```python
import math

import jax
import jax.numpy as jnp
from jax import lax
from jax.experimental import pallas as pl
from jax.experimental.pallas import tpu as pltpu
from jax.sharding import PartitionSpec as P

MESH = pl.DeviceIdType.MESH
BF = jnp.bfloat16
F32 = jnp.float32
I32 = jnp.int32
TR, TC = 768, 384
HALF = TR // 2
KB = 1536
SUB = TR // 4
BLK = 128
ATOM = 8
ITEMS = 128
SLOTS = 256
WIDE = ATOM * BLK + BLK
ATOMS = TR // ATOM
N_COPIES = 224


def kernel(
    zero_hbm, strips, dest, atoms, blocks, patterns, out_zero, out_first,
    a, b, total, part, near, far, rows, sent, came, placed, send_sem, recv_sem, local_sem,
):
    row, col = lax.axis_index("row"), lax.axis_index("col")
    x, core = row // 2, row % 2
    z, y = col // 4, col % 4

    def at(dx=0, dz=0, dy=0, dc=0):
        nx, nz, ny = (lax.rem(x + dx, 4), lax.rem(z + dz, 4), lax.rem(y + dy, 4))
        return {"row": nx * 2 + lax.rem(core + dc, 2), "col": nz * 4 + ny}

    copies, moves, turns, away = {}, {}, {}, {}
    arrived, left = set(), set()

    def send(name, src, dst, device):
        i = len(copies)
        copies[name] = pltpu.make_async_remote_copy(
            src_ref=src, dst_ref=dst, send_sem=send_sem.at[i], recv_sem=recv_sem.at[i],
            device_id=device, device_id_type=MESH,
        )
        copies[name].start()

    def move(name, src, dst):
        moves[name] = pltpu.make_async_copy(src, dst, local_sem.at[len(moves)])
        moves[name].start()

    def got(*names):
        for name in names:
            if name not in arrived:
                arrived.add(name)
                if name[0] == "t":
                    turns[name].wait_recv()
                elif name in copies:
                    copies[name].wait_recv()
                else:
                    moves[name].wait()

    def gone(*names):
        for name in names:
            if name not in left:
                left.add(name)
                if name[0] == "t" and name[3] == 0:
                    pl.when(away[name])(copies[name].wait_send)
                else:
                    copies[name].wait_send()

    def lanes(position):
        return pl.ds(pl.multiple_of(position * TC, BLK), TC)

    def rows_of(position, first=0, size=SUB):
        return pl.ds(pl.multiple_of(position * TC + core * SUB + first, 32), size)

    def rows_at(position, size):
        return pl.ds(pl.multiple_of(position * size, 16), size)

    def tile(u, where=slice(None)):
        return a.at[u, where, lanes(z)]

    def turn(u):
        if u == 0:
            got(("zero",))
        base = len(copies)
        flip = 1 - lax.rem((lax.rem(y - 2 * core + 4, 4) + 1) // 2, 2)
        for i in range(2):
            h = lax.rem(flip + i, 2)
            quarter = 2 * core + h
            k = lax.rem(y - quarter + 4, 4)
            for e in range(2):
                d = lax.rem(core + e, 2)
                src = tile(u, pl.ds(pl.multiple_of(h * TC + d * SUB, 32), SUB))
                dst = b.at[u, k, pl.ds(pl.multiple_of(x * TC + d * SUB, 32), SUB)]
                name = ("t", u, i, e)
                copies[name] = pltpu.make_async_remote_copy(
                    src_ref=src, dst_ref=dst, send_sem=send_sem.at[base + 2 * i + e],
                    recv_sem=recv_sem.at[base + k],
                    device_id={"row": x * 2 + d, "col": z * 4 + quarter}, device_id_type=MESH,
                )
                if e == 0:
                    away[name] = quarter != y
                    pl.when(quarter != y)(copies[name].start)
                    here = pltpu.make_async_copy(src, dst, recv_sem.at[base + k])
                    pl.when(quarter == y)(here.start)
                else:
                    copies[name].start()
        for k in range(4):
            dst = b.at[u, k, rows_of(x)]
            turns["t", u, k] = pltpu.make_async_remote_copy(
                src_ref=dst, dst_ref=dst, send_sem=send_sem.at[base], recv_sem=recv_sem.at[base + k],
                device_id=at(dc=1), device_id_type=MESH,
            )

    def own(u, k):
        got(("t", u, k))
        src = b.at[u, k, rows_of(x)]
        send(("x", u, k, 1), src, src, at(dx=1))
        send(("x", u, k, 3), src, src, at(dx=3))
        send(("c", u, k, 0), src, src, at(dc=1))

    def fwd(u, k, h):
        got(("x", u, k, h))
        source = lax.rem(x + 4 - h, 4)
        src = b.at[u, k, rows_of(source, SUB // 2 if h == 3 else 0, SUB // 2)]
        send(("xx", u, k, h), src, src, at(dx=h))
        src = b.at[u, k, rows_of(source)]
        send(("c", u, k, h), src, src, at(dc=1))

    def last(u, k, h):
        got(("xx", u, k, h))
        src = b.at[u, k, rows_of(lax.rem(x + 2, 4), SUB // 2 if h == 3 else 0, SUB // 2)]
        send(("c", u, k, h + 1), src, src, at(dc=1))

    def side(u):
        if u == 0:
            got(("zero",))
        send(("z", u, 1), tile(u), tile(u), at(dz=1))
        send(("z", u, 3), tile(u), tile(u), at(dz=3))

    def side_on(u, h):
        got(("z", u, h))
        where = pl.ds(HALF if h == 3 else 0, HALF)
        src = a.at[u, where, lanes(lax.rem(z + 4 - h, 4))]
        send(("zz", u, h), src, src, at(dz=h))

    def product(left_unit, right_unit, k):
        got(("z", left_unit, 1), ("z", left_unit, 3), ("zz", left_unit, 1), ("zz", left_unit, 3))
        got(("t", right_unit, k), *(("c", right_unit, k, i) for i in range(5)))
        for h in (1, 3):
            got(("x", right_unit, k, h), ("xx", right_unit, k, h))
        return jnp.dot(a[left_unit], b[right_unit, k], preferred_element_type=F32)

    def sq(s, k):
        total[0, k] = product(2 * s, 2 * s, k)

    def cra(s, k):
        total[1, k] = product(2 * s + 1, 2 * s, k)

    def crb(s, k):
        total[1, k] += product(2 * s, 2 * s + 1, k)

    def far_names(r):
        return [(kind, r, h) for kind in ("s2", "sf", "sd") for h in (1, 3)]

    def send_far(r):
        p = r % 2
        if r > 1:
            gone(*far_names(r - 2))
        part[p, 1] = total[p, 2].astype(BF)
        send(("s2", r, 1), part.at[p, 1, pl.ds(0, HALF)], far.at[r, 0], at(dy=1))
        send(("s2", r, 3), part.at[p, 1, pl.ds(HALF, HALF)], far.at[r, 1], at(dy=3))

    def free(r, h):
        p, i, k = r % 2, h // 2, h
        where = pl.ds(HALF if h == 1 else 0, HALF)
        part[p, 2 * i, where] = total[p, k, where].astype(BF)
        send(("sf", r, h), part.at[p, 2 * i, where], near.at[r, i, where], at(dy=h))

    def dep(r, h):
        p, i, k = r % 2, h // 2, h
        where = pl.ds(0 if h == 1 else HALF, HALF)
        got(("s2", r, h))
        part[p, 2 * i, where] = (total[p, k, where] + far[r, i].astype(F32)).astype(BF)
        send(("sd", r, h), part.at[p, 2 * i, where], near.at[r, i, where], at(dy=h))

    def keep(which, i, j):
        big_row, big_col = row * (TR // BLK) + i, col * (TC // BLK) + j
        return jnp.where(big_row == big_col, 1, patterns[which, big_row, big_col]).astype(F32)

    inv_root = 1.0 / math.sqrt(6144)

    def finish(r):
        p = r % 2
        got(("sf", r, 1), ("sf", r, 3), ("sd", r, 1), ("sd", r, 3))

        @pl.loop(0, TR // BLK)
        def _(i):
            where = pl.ds(pl.multiple_of(i * BLK, BLK), BLK)
            for j in range(TC // BLK):
                cs = slice(j * BLK, (j + 1) * BLK)
                mine = pl.ds(pl.multiple_of(z * TC + j * BLK, BLK), BLK)
                value = (
                    total[p, 0, where, cs]
                    + near[r, 0, where, cs].astype(F32)
                    + near[r, 1, where, cs].astype(F32)
                ) * inv_root
                if r < 2:
                    a[r + 2, where, mine] = (keep(p, i, j) * value).astype(BF)
                else:
                    value = 2.0 * a[r, where, mine].astype(F32) - value
                    out = (out_zero, out_first)[p]
                    out[where, cs] = keep(p, i, j) * value

    def iota(shape, dim):
        return lax.broadcasted_iota(I32, shape, dim)

    def ones(condition):
        return jnp.where(condition, 1.0, 0.0).astype(BF)

    def strips_place():
        named = jnp.broadcast_to(dest[...].astype(F32), (ITEMS, ITEMS))
        square = (ITEMS, ITEMS)
        earlier = (named == named.T) & (iota(square, 1) < iota(square, 0))
        rank = jnp.sum(jnp.where(earlier, 1.0, 0.0), axis=1, keepdims=True).astype(I32)
        d = dest[...]
        place = d * 2 + rank
        atom = jnp.broadcast_to(atoms[...].astype(F32), square).T
        block = jnp.broadcast_to(blocks[...].astype(F32), square).T
        lane = iota(square, 1)
        tags = jnp.where(lane == 0, atom + 1.0, jnp.where(lane == 1, block, 0.0))
        rows[:, : ATOM * BLK] = strips[...]
        rows[:, ATOM * BLK :] = tags.astype(BF)
        spread = ones(iota((ITEMS, SLOTS), 1) == place)
        sent[0] = lax.dot_general(
            spread, rows[...], (((0,), (0,)), ((), ())), preferred_element_type=F32
        ).astype(BF)

    def strips_x():
        mine = rows_at(row, 32)
        for dx in (2, 1, 3, 0):
            for dc in (0, 1):
                if dx or dc:
                    target = lax.rem(x + dx, 4) * 2 + lax.rem(core + dc, 2)
                    src = sent.at[0, rows_at(target, 32)]
                    send(("gx", dx, dc), src, came.at[0, mine], at(dx=dx, dc=dc))
        move(("gx", 0, 0), sent.at[0, mine], came.at[0, mine])

    def strips_col():
        got(*(("gx", dx, dc) for dx in range(4) for dc in range(2)))
        o = iota((SLOTS, SLOTS), 0)
        source = ((o >> 1) & 7) * 32 + (o >> 4) * 2 + (o & 1)
        taken = ones(iota((SLOTS, SLOTS), 1) == source)
        sent[1] = jnp.dot(taken, came[0], preferred_element_type=F32).astype(BF)
        mine = rows_at(col, 16)
        for dz in (2, 1, 3, 0):
            for dy in (2, 1, 3, 0):
                if dz or dy:
                    target = lax.rem(z + dz, 4) * 4 + lax.rem(y + dy, 4)
                    src = sent.at[1, rows_at(target, 16)]
                    send(("gc", dz, dy), src, came.at[1, mine], at(dz=dz, dy=dy))
        move(("gc", 0, 0), sent.at[1, mine], came.at[1, mine])

    def field():
        got(*(("gc", dz, dy) for dz in range(4) for dy in range(4)))
        tags = came[1, :, ATOM * BLK :].astype(F32)
        atom, block = tags[:, 0:1], tags[:, 1:2]
        cell = jnp.where(atom > 0.0, block * ATOMS + atom - 1.0, -1.0)
        placing = ones(iota((SLOTS, TC), 1).astype(F32) == cell)
        summed = lax.dot_general(
            placing, came[1, :, : ATOM * BLK], (((0,), (0,)), ((), ())), preferred_element_type=F32
        )
        for j in range(TC // BLK):
            for i in range(ATOM):
                placed[j, pl.ds(i, ATOMS, stride=ATOM), :] = summed[
                    j * ATOMS : (j + 1) * ATOMS, i * BLK : (i + 1) * BLK
                ]

        @pl.loop(0, TR // BLK)
        def _(i):
            where = pl.ds(pl.multiple_of(i * BLK, BLK), BLK)
            for j in range(TC // BLK):
                mine = pl.ds(pl.multiple_of(z * TC + j * BLK, BLK), BLK)
                value = keep(2, i, j) * placed[j, where, :]
                a[1, where, mine] = (-value).astype(BF)

    move(("zero",), zero_hbm, tile(0))
    peers = [at(dx=dx, dc=dc) for dx in range(4) for dc in range(2) if dx or dc]
    peers += [at(dz=dz, dy=dy) for dz in range(4) for dy in range(4) if dz or dy]
    peers += [at(dy=dy, dc=1) for dy in (1, 2, 3)]
    barrier = pltpu.get_barrier_semaphore()
    for peer in peers:
        pl.semaphore_signal(barrier, inc=1, device_id=peer, device_id_type=MESH)
    strips_place()
    pl.semaphore_wait(barrier, len(peers))

    side(0)
    strips_x()
    turn(0)
    own(0, 2)
    own(0, 3)
    strips_col()
    fwd(0, 2, 1)
    own(0, 1)
    side_on(0, 3)
    side_on(0, 1)
    fwd(0, 2, 3)
    fwd(0, 3, 3)
    fwd(0, 1, 3)
    last(0, 2, 1)
    fwd(0, 3, 1)
    own(0, 0)
    last(0, 2, 3)
    field()
    fwd(0, 1, 1)
    side(1)
    fwd(0, 0, 1)
    turn(1)
    fwd(0, 0, 3)
    own(1, 0)
    last(0, 3, 3)
    sq(0, 2)
    send_far(0)
    last(0, 3, 1)
    last(0, 0, 1)
    own(1, 2)
    fwd(1, 0, 3)
    own(1, 3)
    last(0, 1, 3)
    sq(0, 3)
    last(0, 1, 1)
    fwd(1, 2, 1)
    last(0, 0, 3)
    free(0, 3)
    fwd(1, 2, 3)
    sq(0, 1)
    free(0, 1)
    fwd(1, 3, 1)
    side_on(1, 1)
    side_on(1, 3)
    fwd(1, 0, 1)
    own(1, 1)
    last(1, 2, 1)
    last(1, 2, 3)
    dep(0, 1)
    dep(0, 3)
    last(1, 3, 1)
    sq(0, 0)
    fwd(1, 1, 3)
    fwd(1, 3, 3)
    fwd(1, 1, 1)
    cra(0, 2)
    crb(0, 2)
    send_far(1)
    last(1, 1, 3)
    finish(0)
    side(2)
    last(1, 3, 3)
    cra(0, 3)
    turn(2)
    cra(0, 1)
    crb(0, 3)
    last(1, 0, 1)
    free(1, 3)
    last(1, 1, 1)
    crb(0, 1)
    last(1, 0, 3)
    own(2, 2)
    dep(1, 1)
    own(2, 3)
    free(1, 1)
    dep(1, 3)
    own(2, 1)
    fwd(2, 3, 1)
    side_on(2, 3)
    cra(0, 0)
    fwd(2, 2, 1)
    side_on(2, 1)
    fwd(2, 3, 3)
    crb(0, 0)
    own(2, 0)
    fwd(2, 1, 1)
    fwd(2, 2, 3)
    fwd(2, 1, 3)
    last(2, 2, 1)
    last(2, 3, 1)
    finish(1)
    side(3)
    turn(3)
    last(2, 2, 3)
    fwd(2, 0, 3)
    last(2, 1, 1)
    fwd(2, 0, 1)
    sq(1, 2)
    own(3, 2)
    last(2, 0, 3)
    send_far(2)
    last(2, 3, 3)
    last(2, 1, 3)
    own(3, 1)
    own(3, 3)
    sq(1, 3)
    sq(1, 1)
    free(2, 1)
    fwd(3, 2, 3)
    last(2, 0, 1)
    free(2, 3)
    side_on(3, 1)
    side_on(3, 3)
    fwd(3, 2, 1)
    fwd(3, 1, 1)
    dep(2, 3)
    fwd(3, 3, 3)
    dep(2, 1)
    fwd(3, 1, 3)
    last(3, 2, 3)
    fwd(3, 3, 1)
    sq(1, 0)
    last(3, 3, 3)
    own(3, 0)
    last(3, 1, 1)
    last(3, 3, 1)
    last(3, 1, 3)
    last(3, 2, 1)
    cra(1, 2)
    crb(1, 2)
    send_far(3)
    cra(1, 3)
    crb(1, 3)
    free(3, 3)
    cra(1, 1)
    crb(1, 1)
    free(3, 1)
    cra(1, 0)
    fwd(3, 0, 3)
    dep(3, 3)
    dep(3, 1)
    fwd(3, 0, 1)
    last(3, 0, 3)
    last(3, 0, 1)
    crb(1, 0)
    finish(2)
    finish(3)

    gone(*copies)


def on_device(density, strips, dest_device, atom_slot, block_slot, patterns):
    out = jax.ShapeDtypeStruct((TR, TC), F32)
    vmem = pl.BlockSpec(memory_space=pltpu.VMEM)
    return tuple(pl.pallas_call(
        kernel,
        out_shape=(out, out),
        in_specs=[
            pl.BlockSpec(memory_space=pl.ANY), vmem, vmem, vmem, vmem,
            pl.BlockSpec(memory_space=pltpu.SMEM),
        ],
        out_specs=(vmem, vmem),
        scratch_shapes=[
            pltpu.VMEM((4, TR, KB), BF),
            pltpu.VMEM((4, 4, KB, TC), BF),
            pltpu.VMEM((2, 4, TR, TC), F32),
            pltpu.VMEM((2, 3, TR, TC), BF),
            pltpu.VMEM((4, 2, TR, TC), BF),
            pltpu.VMEM((4, 2, HALF, TC), BF),
            pltpu.VMEM((ITEMS, WIDE), BF),
            pltpu.VMEM((2, SLOTS, WIDE), BF),
            pltpu.VMEM((2, SLOTS, WIDE), BF),
            pltpu.VMEM((TC // BLK, TR, BLK), F32),
            pltpu.SemaphoreType.DMA((N_COPIES,)),
            pltpu.SemaphoreType.DMA((N_COPIES,)),
            pltpu.SemaphoreType.DMA((16,)),
        ],
        compiler_params=pltpu.CompilerParams(
            collective_id=0, has_side_effects=True, vmem_limit_bytes=62 * 2**20 - 2**19
        ),
        cost_estimate=pl.CostEstimate(flops=21743271936, bytes_accessed=8 * 2**20, transcendentals=0),
    )(
        density,
        strips.reshape(ITEMS, ATOM * BLK),
        dest_device,
        atom_slot.reshape(1, ITEMS),
        block_slot.reshape(1, ITEMS),
        patterns,
    ))


def solution(mesh):
    return jax.shard_map(
        on_device,
        mesh=mesh,
        in_specs=(
            P("row", "col"),
            P(("row", "col"), None, None),
            P(("row", "col"), None),
            P(("row", "col")),
            P(("row", "col")),
            P(),
        ),
        out_specs=(P("row", "col"), P("row", "col")),
        check_vma=False,
    )
```

time: 175 us -> 156 us (0.89)
  Pallas kernels: 167 us -> 148 us
    pallas_call x1, Pallas kernels: 167 us -> 148 us  [on_device(): pl.pallas_call(kernel, out_shape=(out, out), in_specs=[pl.BlockSpec(memor...]
where the time goes in v4:
time: 156 us; the launch traced here: 155 us
  Pallas kernels  148 us (95%)
  local copies, waits for them, and re-layouts  6.56 us (4%)
    pallas_call x1, Pallas kernels, on_device(): pl.pallas_call(kernel, out_shape=(out, out), in_specs=[pl.BlockSpec(memor...  148 us
    unnamed x6, local copies, waits for them, and re-layouts  6.56 us

profile of v4, /device:TPU:1, one launch (start us, length us, event | category | flops | bytes accessed | tf_op | source)
XLA Modules:
  0.0 155.0 jit_solution(3469021708237466678)
XLA Ops:
  0.6 1.4 copy.8.dest
  2.0 1.7 %copy.11 = bf16[16,8,8,128]{3,1,2,0:T(8,128)(2,1)} copy(bf16[16,8,8,128]{3,2,1,0:T(8,128)(2,1)} %bitcast.6) | data formatting | bytes 524288
  3.7 147.8 %shard_map.77 = (f32[768,384]{1,0:T(8,128)}, f32[768,384]{1,0:T(8,128)}) custom-call(bf16[768,384]{1,0:T(8,128)(2,1)} %zero_hbm.1, bf16[128,1024]{1,0:T(8,128)(2,1)} %bitcast.7, s32[128,1]{1,0:T(8,128)} %copy.8.dest, s32[1,128]{1,0:T(1,128)} %bitcast.8, s32[1,128]{1,0:T(1,128)} %bitcast.9, s32[3,48,48]{2,1,0:T(8,128)} %patterns.1), custom_call_target="tpu_custom_call" | custom-call | flops 21743271936 | bytes 8388608 | tf_op jit(solution)/shard_map/pallas_call | solution.py:455
  151.5 0.0 copy-start
  151.5 2.5 %copy.14 = f32[768,384]{1,0:T(8,128)} copy(f32[768,384]{1,0:T(8,128)} %get-tuple-element.4) | data formatting | bytes 2359296
  154.0 0.0 copy-done
  154.0 1.0 copy.15
Async XLA Ops:
  151.5 2.5 %copy-start = (f32[768,384]{1,0:T(8,128)S(1)}, f32[768,384]{1,0:T(8,128)}, u32[]{:S(2)}) copy-start(f32[768,384]{1,0:T(8,128)} %get-tuple-element.5) | copy-start | bytes 3538948

commit v5 on v4

v5 whole, which is shorter than its diff:
```python
import math

import jax
import jax.numpy as jnp
from jax import lax
from jax.experimental import pallas as pl
from jax.experimental.pallas import tpu as pltpu
from jax.sharding import PartitionSpec as P

MESH = pl.DeviceIdType.MESH
BF = jnp.bfloat16
F32 = jnp.float32
I32 = jnp.int32
TR, TC = 768, 384
HALF = TR // 2
KB = 1536
SUB = TR // 4
BLK = 128
ATOM = 8
ITEMS = 128
SLOTS = 256
WIDE = ATOM * BLK + BLK
ATOMS = TR // ATOM
N_COPIES = 256


def kernel(
    zero_hbm, strips_hbm, dest, atoms, blocks, patterns_hbm, out_zero, out_first,
    a, b, total, part, near, far, rows, sent, came, placed, strips, patterns, send_sem, recv_sem, local_sem,
):
    row, col = lax.axis_index("row"), lax.axis_index("col")
    x, core = row // 2, row % 2
    z, y = col // 4, col % 4

    def at(dx=0, dz=0, dy=0, dc=0):
        nx, nz, ny = (lax.rem(x + dx, 4), lax.rem(z + dz, 4), lax.rem(y + dy, 4))
        return {"row": nx * 2 + lax.rem(core + dc, 2), "col": nz * 4 + ny}

    copies, moves, turns, bases, away = {}, {}, {}, {}, {}
    arrived, left = set(), set()
    used = [0]

    def take(n):
        used[0] += n
        return used[0] - n

    def send(name, src, dst, device):
        i = take(1)
        copies[name] = pltpu.make_async_remote_copy(
            src_ref=src, dst_ref=dst, send_sem=send_sem.at[i], recv_sem=recv_sem.at[i],
            device_id=device, device_id_type=MESH,
        )
        copies[name].start()

    def move(name, src, dst):
        moves[name] = pltpu.make_async_copy(src, dst, local_sem.at[len(moves)])
        moves[name].start()

    def got(*names):
        for name in names:
            if name not in arrived:
                arrived.add(name)
                if name[0] == "t":
                    turns[name].wait_recv()
                elif name in copies:
                    copies[name].wait_recv()
                else:
                    moves[name].wait()

    def gone(*names):
        for name in names:
            if name not in left:
                left.add(name)
                if name[0] == "t" and name[3] == 0:
                    pl.when(away[name])(copies[name].wait_send)
                else:
                    copies[name].wait_send()

    def lanes(position):
        return pl.ds(pl.multiple_of(position * TC, BLK), TC)

    def rows_of(position, first=0, size=SUB):
        return pl.ds(pl.multiple_of(position * TC + core * SUB + first, 32), size)

    def rows_at(position, size):
        return pl.ds(pl.multiple_of(position * size, 16), size)

    def tile(u, where=slice(None)):
        return a.at[u, where, lanes(z)]

    def turn(u, hh):
        if u == 0:
            got(("zero",))
        if ("t", u, 0) not in turns:
            base = take(4)
            for k in range(4):
                dst = b.at[u, k, rows_of(x)]
                turns["t", u, k] = pltpu.make_async_remote_copy(
                    src_ref=dst, dst_ref=dst, send_sem=send_sem.at[base],
                    recv_sem=recv_sem.at[base + k], device_id=at(dc=1), device_id_type=MESH,
                )
            bases[u] = base
        base = bases[u]
        quarter = 2 * core + hh
        k = lax.rem(y - quarter + 4, 4)
        for e in (1, 0):
            d = lax.rem(core + e, 2)
            src = tile(u, pl.ds(pl.multiple_of(hh * TC + d * SUB, 32), SUB))
            dst = b.at[u, k, pl.ds(pl.multiple_of(x * TC + d * SUB, 32), SUB)]
            name = ("t", u, hh, e)
            copies[name] = pltpu.make_async_remote_copy(
                src_ref=src, dst_ref=dst, send_sem=send_sem.at[base + 2 * hh + e],
                recv_sem=recv_sem.at[base + k],
                device_id={"row": x * 2 + d, "col": z * 4 + quarter}, device_id_type=MESH,
            )
            if e == 0:
                away[name] = quarter != y
                pl.when(quarter != y)(copies[name].start)
                here = pltpu.make_async_copy(src, dst, recv_sem.at[base + k])
                pl.when(quarter == y)(here.start)
            else:
                copies[name].start()

    def own(u, k):
        got(("t", u, k))
        src = b.at[u, k, rows_of(x)]
        send(("x", u, k, 1), src, src, at(dx=1))
        send(("x", u, k, 3), src, src, at(dx=3))
        send(("c", u, k, 0), src, src, at(dc=1))

    def fwd(u, k, h):
        got(("x", u, k, h))
        source = lax.rem(x + 4 - h, 4)
        src = b.at[u, k, rows_of(source, SUB // 2 if h == 3 else 0, SUB // 2)]
        send(("xx", u, k, h), src, src, at(dx=h))
        src = b.at[u, k, rows_of(source)]
        send(("c", u, k, h), src, src, at(dc=1))

    def last(u, k, h):
        got(("xx", u, k, h))
        src = b.at[u, k, rows_of(lax.rem(x + 2, 4), SUB // 2 if h == 3 else 0, SUB // 2)]
        send(("c", u, k, h + 1), src, src, at(dc=1))

    def side(u, hh):
        if u == 0:
            got(("zero",))
        src = tile(u, pl.ds(hh * HALF, HALF))
        send(("z", u, hh, 1), src, src, at(dz=1))
        send(("z", u, hh, 3), src, src, at(dz=3))

    def side_on(u, hh, h):
        got(("z", u, hh, h))
        where = pl.ds(hh * HALF + (SUB if h == 3 else 0), SUB)
        src = a.at[u, where, lanes(lax.rem(z + 4 - h, 4))]
        send(("zz", u, hh, h), src, src, at(dz=h))

    def half_rows(hh):
        return pl.ds(hh * HALF, HALF)

    def product(left_unit, right_unit, k, hh):
        for h in (1, 3):
            got(("z", left_unit, hh, h), ("zz", left_unit, hh, h))
            got(("x", right_unit, k, h), ("xx", right_unit, k, h))
        got(("t", right_unit, k), *(("c", right_unit, k, i) for i in range(5)))
        return jnp.dot(a[left_unit, half_rows(hh)], b[right_unit, k], preferred_element_type=F32)

    def sq(s, k, hh):
        total[0, k, half_rows(hh)] = product(2 * s, 2 * s, k, hh)

    def cra(s, k, hh):
        total[1, k, half_rows(hh)] = product(2 * s + 1, 2 * s, k, hh)

    def crb(s, k, hh):
        total[1, k, half_rows(hh)] += product(2 * s, 2 * s + 1, k, hh)

    def reuse(kind, r, h):
        if r > 1:
            gone((kind, r - 2, h))

    def send_far(r, hh):
        p, h, where = r % 2, 2 * hh + 1, half_rows(hh)
        reuse("s2", r, h)
        part[p, 1, where] = total[p, 2, where].astype(BF)
        send(("s2", r, h), part.at[p, 1, where], far.at[r, hh], at(dy=h))

    def free(r, h):
        p, i, where = r % 2, h // 2, half_rows(1 - h // 2)
        reuse("sf", r, h)
        part[p, 2 * i, where] = total[p, h, where].astype(BF)
        send(("sf", r, h), part.at[p, 2 * i, where], near.at[r, i, where], at(dy=h))

    def dep(r, h):
        p, i, where = r % 2, h // 2, half_rows(h // 2)
        reuse("sd", r, h)
        got(("s2", r, h))
        part[p, 2 * i, where] = (total[p, h, where] + far[r, i].astype(F32)).astype(BF)
        send(("sd", r, h), part.at[p, 2 * i, where], near.at[r, i, where], at(dy=h))

    def keep(which, i, j):
        big_row, big_col = row * (TR // BLK) + i, col * (TC // BLK) + j
        return jnp.where(big_row == big_col, 1, patterns[which, big_row, big_col]).astype(F32)

    inv_root = 1.0 / math.sqrt(6144)

    def finish(r, hh):
        got(("patterns",))
        p = r % 2
        got(("sd" if hh == 0 else "sf", r, 1), ("sf" if hh == 0 else "sd", r, 3))

        @pl.loop(hh * (HALF // BLK), (hh + 1) * (HALF // BLK))
        def _(i):
            where = pl.ds(pl.multiple_of(i * BLK, BLK), BLK)
            for j in range(TC // BLK):
                cs = slice(j * BLK, (j + 1) * BLK)
                mine = pl.ds(pl.multiple_of(z * TC + j * BLK, BLK), BLK)
                value = (
                    total[p, 0, where, cs]
                    + near[r, 0, where, cs].astype(F32)
                    + near[r, 1, where, cs].astype(F32)
                ) * inv_root
                if r < 2:
                    a[r + 2, where, mine] = (keep(p, i, j) * value).astype(BF)
                else:
                    value = 2.0 * a[r, where, mine].astype(F32) - value
                    out = (out_zero, out_first)[p]
                    out[where, cs] = keep(p, i, j) * value

    def iota(shape, dim):
        return lax.broadcasted_iota(I32, shape, dim)

    def ones(condition):
        return jnp.where(condition, 1.0, 0.0).astype(BF)

    def strips_place():
        square = (ITEMS, ITEMS)

        def across(ref):
            return jnp.broadcast_to(ref[...].astype(F32), square)

        named, own_name = across(dest), across(dest).T
        earlier = (named == own_name) & (iota(square, 1) < iota(square, 0))
        rank = jnp.sum(jnp.where(earlier, 1.0, 0.0), axis=1, keepdims=True)
        place = (own_name[:, 0:1] * 2.0 + rank).astype(I32)
        lane = iota(square, 1)
        tags = jnp.where(
            lane == 0, across(atoms).T + 1.0, jnp.where(lane == 1, across(blocks).T, 0.0)
        )
        rows[:, ATOM * BLK :] = tags.astype(BF)
        spread = ones(iota((ITEMS, SLOTS), 1) == place)
        got(("strips",))
        placed[0 : ITEMS * ATOM] = strips[...].astype(F32)
        for i in range(ATOM):
            lines = placed[pl.ds(i, ITEMS, stride=ATOM), :]
            rows[:, i * BLK : (i + 1) * BLK] = lines.astype(BF)
        sent[0] = lax.dot_general(
            spread, rows[...], (((0,), (0,)), ((), ())), preferred_element_type=F32
        ).astype(BF)

    def strips_x():
        mine = rows_at(row, 32)
        for dx in (2, 1, 3, 0):
            for dc in (0, 1):
                if dx or dc:
                    target = lax.rem(x + dx, 4) * 2 + lax.rem(core + dc, 2)
                    src = sent.at[0, rows_at(target, 32)]
                    send(("gx", dx, dc), src, came.at[0, mine], at(dx=dx, dc=dc))
        move(("gx", 0, 0), sent.at[0, mine], came.at[0, mine])

    def strips_col():
        got(*(("gx", dx, dc) for dx in range(4) for dc in range(2)))
        o = iota((SLOTS, SLOTS), 0)
        source = ((o >> 1) & 7) * 32 + (o >> 4) * 2 + (o & 1)
        taken = ones(iota((SLOTS, SLOTS), 1) == source)
        sent[1] = jnp.dot(taken, came[0], preferred_element_type=F32).astype(BF)
        mine = rows_at(col, 16)
        for dz in (2, 1, 3, 0):
            for dy in (2, 1, 3, 0):
                if dz or dy:
                    target = lax.rem(z + dz, 4) * 4 + lax.rem(y + dy, 4)
                    src = sent.at[1, rows_at(target, 16)]
                    send(("gc", dz, dy), src, came.at[1, mine], at(dz=dz, dy=dy))
        move(("gc", 0, 0), sent.at[1, mine], came.at[1, mine])

    def field():
        got(("patterns",))
        got(*(("gc", dz, dy) for dz in range(4) for dy in range(4)))
        tags = came[1, :, ATOM * BLK :].astype(F32)
        atom, block = tags[:, 0:1], tags[:, 1:2]
        cell = jnp.where(atom > 0.0, block * ATOMS + atom - 1.0, -1.0)
        placing = ones(iota((SLOTS, TC), 1).astype(F32) == cell)
        summed = lax.dot_general(
            placing, came[1, :, : ATOM * BLK], (((0,), (0,)), ((), ())), preferred_element_type=F32
        )
        for j in range(TC // BLK):
            for i in range(ATOM):
                placed[pl.ds(j * TR + i, ATOMS, stride=ATOM), :] = summed[
                    j * ATOMS : (j + 1) * ATOMS, i * BLK : (i + 1) * BLK
                ]

        @pl.loop(0, TR // BLK)
        def _(i):
            where = pl.ds(pl.multiple_of(i * BLK, BLK), BLK)
            for j in range(TC // BLK):
                mine = pl.ds(pl.multiple_of(z * TC + j * BLK, BLK), BLK)
                value = keep(2, i, j) * placed[pl.ds(pl.multiple_of(j * TR + i * BLK, BLK), BLK), :]
                a[1, where, mine] = (-value).astype(BF)

    move(("strips",), strips_hbm, strips)
    move(("zero",), zero_hbm, tile(0))
    move(("patterns",), patterns_hbm, patterns)
    peers = [at(dx=dx, dc=dc) for dx in range(4) for dc in range(2) if dx or dc]
    peers += [at(dz=dz, dy=dy) for dz in range(4) for dy in range(4) if dz or dy]
    peers += [at(dy=dy, dc=1) for dy in (1, 2, 3)]
    barrier = pltpu.get_barrier_semaphore()
    for peer in peers:
        pl.semaphore_signal(barrier, inc=1, device_id=peer, device_id_type=MESH)
    strips_place()
    pl.semaphore_wait(barrier, len(peers))

    strips_x()
    turn(0, 1)
    side(0, 0)
    turn(0, 0)
    strips_col()
    own(0, 2)
    own(0, 1)
    side(0, 1)
    own(0, 3)
    fwd(0, 1, 1)
    side_on(0, 0, 1)
    fwd(0, 2, 1)
    fwd(0, 2, 3)
    own(0, 0)
    field()
    turn(1, 0)
    side_on(0, 0, 3)
    side_on(0, 1, 1)
    fwd(0, 1, 3)
    fwd(0, 3, 3)
    turn(1, 1)
    last(0, 2, 1)
    last(0, 2, 3)
    fwd(0, 3, 1)
    side_on(0, 1, 3)
    sq(0, 2, 0)
    fwd(0, 0, 1)
    send_far(0, 0)
    last(0, 1, 1)
    side(1, 0)
    last(0, 1, 3)
    last(0, 3, 3)
    last(0, 3, 1)
    own(1, 2)
    fwd(0, 0, 3)
    sq(0, 2, 1)
    send_far(0, 1)
    sq(0, 1, 1)
    sq(0, 1, 0)
    own(1, 1)
    fwd(1, 2, 1)
    side(1, 1)
    sq(0, 3, 0)
    dep(0, 1)
    free(0, 3)
    own(1, 0)
    sq(0, 3, 1)
    fwd(1, 1, 3)
    last(0, 0, 1)
    fwd(1, 2, 3)
    free(0, 1)
    side_on(1, 0, 3)
    dep(0, 3)
    side_on(1, 0, 1)
    own(1, 3)
    last(0, 0, 3)
    sq(0, 0, 1)
    fwd(1, 1, 1)
    last(1, 2, 1)
    sq(0, 0, 0)
    side_on(1, 1, 1)
    fwd(1, 3, 1)
    last(1, 1, 3)
    cra(0, 3, 0)
    side_on(1, 1, 3)
    fwd(1, 0, 1)
    cra(0, 2, 0)
    fwd(1, 0, 3)
    last(1, 2, 3)
    finish(0, 0)
    turn(2, 0)
    side(2, 0)
    fwd(1, 3, 3)
    last(1, 3, 1)
    crb(0, 2, 0)
    last(1, 1, 1)
    finish(0, 1)
    turn(2, 1)
    send_far(1, 0)
    cra(0, 1, 1)
    last(1, 3, 3)
    cra(0, 2, 1)
    cra(0, 3, 1)
    crb(0, 2, 1)
    last(1, 0, 1)
    send_far(1, 1)
    crb(0, 1, 1)
    own(2, 3)
    own(2, 2)
    cra(0, 1, 0)
    side(2, 1)
    cra(0, 0, 1)
    own(2, 1)
    crb(0, 1, 0)
    crb(0, 3, 0)
    free(1, 3)
    side_on(2, 0, 1)
    dep(1, 1)
    side_on(2, 0, 3)
    fwd(2, 2, 3)
    cra(0, 0, 0)
    fwd(2, 3, 3)
    own(2, 0)
    crb(0, 3, 1)
    fwd(2, 2, 1)
    free(1, 1)
    fwd(2, 3, 1)
    dep(1, 3)
    last(1, 0, 3)
    side_on(2, 1, 3)
    side_on(2, 1, 1)
    crb(0, 0, 1)
    fwd(2, 1, 3)
    fwd(2, 1, 1)
    crb(0, 0, 0)
    finish(1, 0)
    turn(3, 0)
    last(2, 3, 3)
    side(3, 0)
    last(2, 2, 3)
    last(2, 2, 1)
    sq(1, 2, 0)
    sq(1, 2, 1)
    fwd(2, 0, 3)
    last(2, 3, 1)
    last(2, 1, 3)
    last(2, 1, 1)
    finish(1, 1)
    turn(3, 1)
    send_far(2, 0)
    fwd(2, 0, 1)
    side(3, 1)
    sq(1, 1, 1)
    send_far(2, 1)
    own(3, 2)
    free(2, 1)
    side_on(3, 0, 3)
    sq(1, 3, 0)
    own(3, 3)
    side_on(3, 0, 1)
    free(2, 3)
    sq(1, 1, 0)
    sq(1, 3, 1)
    fwd(3, 2, 3)
    side_on(3, 1, 3)
    dep(2, 3)
    fwd(3, 2, 1)
    last(2, 0, 1)
    own(3, 1)
    cra(1, 2, 0)
    side_on(3, 1, 1)
    cra(1, 1, 0)
    dep(2, 1)
    fwd(3, 3, 1)
    cra(1, 3, 0)
    last(3, 2, 1)
    last(3, 2, 3)
    own(3, 0)
    crb(1, 2, 0)
    fwd(3, 3, 3)
    fwd(3, 1, 1)
    cra(1, 2, 1)
    cra(1, 3, 1)
    last(2, 0, 3)
    crb(1, 2, 1)
    send_far(3, 1)
    fwd(3, 1, 3)
    send_far(3, 0)
    last(3, 3, 1)
    cra(1, 1, 1)
    last(3, 3, 3)
    fwd(3, 0, 3)
    crb(1, 3, 0)
    last(3, 1, 1)
    last(3, 1, 3)
    sq(1, 0, 1)
    free(3, 3)
    crb(1, 3, 1)
    crb(1, 1, 1)
    free(3, 1)
    fwd(3, 0, 1)
    crb(1, 1, 0)
    sq(1, 0, 0)
    cra(1, 0, 0)
    finish(2, 1)
    cra(1, 0, 1)
    last(3, 0, 3)
    last(3, 0, 1)
    dep(3, 1)
    dep(3, 3)
    finish(2, 0)
    crb(1, 0, 1)
    crb(1, 0, 0)
    finish(3, 1)
    finish(3, 0)

    gone(*copies)


def hand_on(zero, first, out_zero, out_first, sem):
    copies = []
    for i in range(4):
        where = pl.ds(i * SUB, SUB)
        for src, dst in ((zero, out_zero), (first, out_first)):
            copies.append(pltpu.make_async_copy(src.at[where], dst.at[where], sem.at[len(copies)]))
            copies[-1].start()
    for copy in copies:
        copy.wait()


def on_device(density, strips, dest_device, atom_slot, block_slot, patterns):
    out = jax.ShapeDtypeStruct((TR, TC), F32)
    vmem = pl.BlockSpec(memory_space=pltpu.VMEM)
    hbm = pl.BlockSpec(memory_space=pl.ANY)
    results = pl.pallas_call(
        kernel,
        out_shape=(out, out),
        in_specs=[
            hbm, hbm, vmem, vmem, vmem, hbm,
        ],
        out_specs=(vmem, vmem),
        scratch_shapes=[
            pltpu.VMEM((4, TR, KB), BF),
            pltpu.VMEM((4, 4, KB, TC), BF),
            pltpu.VMEM((2, 4, TR, TC), F32),
            pltpu.VMEM((2, 3, TR, TC), BF),
            pltpu.VMEM((4, 2, TR, TC), BF),
            pltpu.VMEM((4, 2, HALF, TC), BF),
            pltpu.VMEM((ITEMS, WIDE), BF),
            pltpu.VMEM((2, SLOTS, WIDE), BF),
            pltpu.VMEM((2, SLOTS, WIDE), BF),
            pltpu.VMEM((TC // BLK * TR, BLK), F32),
            pltpu.VMEM((ITEMS * ATOM, BLK), BF),
            pltpu.SMEM((3, 48, 48), I32),
            pltpu.SemaphoreType.DMA((N_COPIES,)),
            pltpu.SemaphoreType.DMA((N_COPIES,)),
            pltpu.SemaphoreType.DMA((16,)),
        ],
        compiler_params=pltpu.CompilerParams(
            collective_id=0, has_side_effects=True, vmem_limit_bytes=62 * 2**20 - 2**19
        ),
        cost_estimate=pl.CostEstimate(flops=21743271936, bytes_accessed=8 * 2**20, transcendentals=0),
    )(
        density,
        strips.reshape(ITEMS * ATOM, BLK),
        dest_device.reshape(1, ITEMS),
        atom_slot.reshape(1, ITEMS),
        block_slot.reshape(1, ITEMS),
        patterns,
    )
    return tuple(pl.pallas_call(
        hand_on,
        out_shape=(out, out),
        in_specs=(hbm, hbm),
        out_specs=(hbm, hbm),
        scratch_shapes=[pltpu.SemaphoreType.DMA((8,))],
    )(*results))


def solution(mesh):
    return jax.shard_map(
        on_device,
        mesh=mesh,
        in_specs=(
            P("row", "col"),
            P(("row", "col"), None, None),
            P(("row", "col"), None),
            P(("row", "col")),
            P(("row", "col")),
            P(),
        ),
        out_specs=(P("row", "col"), P("row", "col")),
        check_vma=False,
    )
```

time: 156 us -> 218 us (1.40)
  Pallas kernels: 148 us -> 217 us
  local copies, waits for them, and re-layouts: 6.56 us -> 0 us
    pallas_call x1 -> x2, Pallas kernels: 148 us -> 217 us  [the longest x1 145 us: on_device(): pl.pallas_call(kernel, out_shape=(out, out), in_specs=[hbm, hbm, vmem, vm...]
    unnamed x6 -> x0, local copies, waits for them, and re-layouts: 6.56 us -> none
where the time goes in v5:
time: 218 us
  Pallas kernels  217 us (100%)
    pallas_call x1, Pallas kernels, on_device(): pl.pallas_call(kernel, out_shape=(out, out), in_specs=[hbm, hbm, vmem, vm...  145 us
    pallas_call x1, Pallas kernels, on_device(): pl.pallas_call(hand_on, out_shape=(out, out), in_specs=(hbm, hbm), out_sp...  72.6 us

profile of v5, /device:TPU:1, one launch (start us, length us, event | category | flops | bytes accessed | tf_op | source)
XLA Modules:
  0.0 218.2 jit_solution(13125601062412343466)
XLA Ops:
  0.6 144.7 %shard_map.77 = (f32[768,384]{1,0:T(8,128)}, f32[768,384]{1,0:T(8,128)}) custom-call(bf16[768,384]{1,0:T(8,128)(2,1)} %zero_hbm.1, bf16[1024,128]{1,0:T(8,128)(2,1)} %bitcast.4, s32[1,128]{1,0:T(1,128)} %bitcast.5, s32[1,128]{1,0:T(1,128)} %bitcast.6, s32[1,128]{1,0:T(1,128)} %bitcast.7, s32[3,48,48]{2,1,0:T(8,128)} %patterns_hbm.1), custom_call_target="tpu_custom_call" | custom-call | flops 21743271936 | bytes 8388608 | tf_op jit(solution)/shard_map/pallas_call | solution.py:534
  145.3 72.6 %shard_map.78 = (f32[768,384]{1,0:T(8,128)}, f32[768,384]{1,0:T(8,128)}) custom-call(f32[768,384]{1,0:T(8,128)} %get-tuple-element.4.zero, f32[768,384]{1,0:T(8,128)} %get-tuple-element.5.first), custom_call_target="tpu_custom_call" | custom-call | tf_op jit(solution)/shard_map/pallas_call | solution.py:570

commit v6 on v5

--- a/solution.py
+++ b/solution.py
@@ -21,12 +21,12 @@
 SLOTS = 256
 WIDE = ATOM * BLK + BLK
 ATOMS = TR // ATOM
-N_COPIES = 256
+N_COPIES = 272
 
 
 def kernel(
     zero_hbm, strips_hbm, dest, atoms, blocks, patterns_hbm, out_zero, out_first,
-    a, b, total, part, near, far, rows, sent, came, placed, strips, patterns, send_sem, recv_sem, local_sem,
+    a, b, total, part, near, far, rows, sent, came, placed, strips, patterns, out, send_sem, recv_sem, local_sem,
 ):
     row, col = lax.axis_index("row"), lax.axis_index("col")
     x, core = row // 2, row % 2
@@ -173,28 +173,31 @@
     def crb(s, k, hh):
         total[1, k, half_rows(hh)] += product(2 * s, 2 * s + 1, k, hh)
 
-    def reuse(kind, r, h):
+    def reuse(kind, r, hh, h):
         if r > 1:
-            gone((kind, r - 2, h))
+            gone((kind, r - 2, hh, h))
 
     def send_far(r, hh):
-        p, h, where = r % 2, 2 * hh + 1, half_rows(hh)
-        reuse("s2", r, h)
+        p, where = r % 2, half_rows(hh)
+        for h in (1, 3):
+            reuse("s2", r, hh, h)
         part[p, 1, where] = total[p, 2, where].astype(BF)
-        send(("s2", r, h), part.at[p, 1, where], far.at[r, hh], at(dy=h))
-
-    def free(r, h):
-        p, i, where = r % 2, h // 2, half_rows(1 - h // 2)
-        reuse("sf", r, h)
+        for h in (1, 3):
+            where = pl.ds(hh * HALF + h // 2 * SUB, SUB)
+            send(("s2", r, hh, h), part.at[p, 1, where], far.at[r, where], at(dy=h))
+
+    def free(r, hh, h):
+        p, i, where = r % 2, h // 2, pl.ds(hh * HALF + (1 - h // 2) * SUB, SUB)
+        reuse("sf", r, hh, h)
         part[p, 2 * i, where] = total[p, h, where].astype(BF)
-        send(("sf", r, h), part.at[p, 2 * i, where], near.at[r, i, where], at(dy=h))
-
-    def dep(r, h):
-        p, i, where = r % 2, h // 2, half_rows(h // 2)
-        reuse("sd", r, h)
-        got(("s2", r, h))
-        part[p, 2 * i, where] = (total[p, h, where] + far[r, i].astype(F32)).astype(BF)
-        send(("sd", r, h), part.at[p, 2 * i, where], near.at[r, i, where], at(dy=h))
+        send(("sf", r, hh, h), part.at[p, 2 * i, where], near.at[r, i, where], at(dy=h))
+
+    def dep(r, hh, h):
+        p, i, where = r % 2, h // 2, pl.ds(hh * HALF + h // 2 * SUB, SUB)
+        reuse("sd", r, hh, h)
+        got(("s2", r, hh, h))
+        part[p, 2 * i, where] = (total[p, h, where] + far[r, where].astype(F32)).astype(BF)
+        send(("sd", r, hh, h), part.at[p, 2 * i, where], near.at[r, i, where], at(dy=h))
 
     def keep(which, i, j):
         big_row, big_col = row * (TR // BLK) + i, col * (TC // BLK) + j
@@ -205,7 +208,7 @@
     def finish(r, hh):
         got(("patterns",))
         p = r % 2
-        got(("sd" if hh == 0 else "sf", r, 1), ("sf" if hh == 0 else "sd", r, 3))
+        got(*((kind, r, hh, h) for kind in ("sf", "sd") for h in (1, 3)))
 
         @pl.loop(hh * (HALF // BLK), (hh + 1) * (HALF // BLK))
         def _(i):
@@ -222,8 +225,11 @@
                     a[r + 2, where, mine] = (keep(p, i, j) * value).astype(BF)
                 else:
                     value = 2.0 * a[r, where, mine].astype(F32) - value
-                    out = (out_zero, out_first)[p]
-                    out[where, cs] = keep(p, i, j) * value
+                    out[p, where, cs] = keep(p, i, j) * value
+
+        if r > 1:
+            where = half_rows(hh)
+            move(("out", p, hh), out.at[p, where], (out_zero, out_first)[p].at[where])
 
     def iota(shape, dim):
         return lax.broadcasted_iota(I32, shape, dim)
@@ -319,212 +325,234 @@
 
     strips_x()
     turn(0, 1)
-    side(0, 0)
+    side(0, 1)
     turn(0, 0)
     strips_col()
+    side(0, 0)
+    own(0, 3)
+    side_on(0, 1, 1)
     own(0, 2)
+    side_on(0, 1, 3)
     own(0, 1)
-    side(0, 1)
-    own(0, 3)
-    fwd(0, 1, 1)
-    side_on(0, 0, 1)
+    fwd(0, 3, 3)
     fwd(0, 2, 1)
     fwd(0, 2, 3)
+    field()
     own(0, 0)
-    field()
     turn(1, 0)
+    fwd(0, 1, 1)
+    last(0, 2, 1)
+    last(0, 3, 3)
     side_on(0, 0, 3)
-    side_on(0, 1, 1)
+    turn(1, 1)
     fwd(0, 1, 3)
-    fwd(0, 3, 3)
-    turn(1, 1)
-    last(0, 2, 1)
+    fwd(0, 3, 1)
+    side_on(0, 0, 1)
     last(0, 2, 3)
-    fwd(0, 3, 1)
-    side_on(0, 1, 3)
+    fwd(0, 0, 1)
+    sq(0, 2, 1)
+    send_far(0, 1)
+    side(1, 1)
+    side(1, 0)
+    fwd(0, 0, 3)
+    last(0, 1, 3)
+    own(1, 2)
+    last(0, 3, 1)
+    own(1, 1)
     sq(0, 2, 0)
-    fwd(0, 0, 1)
     send_far(0, 0)
     last(0, 1, 1)
-    side(1, 0)
-    last(0, 1, 3)
-    last(0, 3, 3)
-    last(0, 3, 1)
-    own(1, 2)
-    fwd(0, 0, 3)
-    sq(0, 2, 1)
-    send_far(0, 1)
+    sq(0, 3, 1)
+    last(0, 0, 1)
+    sq(0, 3, 0)
+    sq(0, 1, 0)
+    free(0, 0, 3)
+    free(0, 0, 1)
+    dep(0, 1, 3)
     sq(0, 1, 1)
-    sq(0, 1, 0)
-    own(1, 1)
-    fwd(1, 2, 1)
-    side(1, 1)
-    sq(0, 3, 0)
-    dep(0, 1)
-    free(0, 3)
-    own(1, 0)
-    sq(0, 3, 1)
-    fwd(1, 1, 3)
-    last(0, 0, 1)
-    fwd(1, 2, 3)
-    free(0, 1)
-    side_on(1, 0, 3)
-    dep(0, 3)
-    side_on(1, 0, 1)
     own(1, 3)
     last(0, 0, 3)
+    free(0, 1, 1)
+    dep(0, 0, 1)
+    fwd(1, 1, 1)
+    fwd(1, 2, 3)
+    dep(0, 0, 3)
+    fwd(1, 2, 1)
+    sq(0, 0, 0)
+    free(0, 1, 3)
+    side_on(1, 1, 3)
+    fwd(1, 1, 3)
+    side_on(1, 1, 1)
+    own(1, 0)
+    dep(0, 1, 1)
+    side_on(1, 0, 3)
+    last(1, 2, 3)
+    last(1, 1, 1)
+    fwd(1, 3, 1)
     sq(0, 0, 1)
-    fwd(1, 1, 1)
+    side_on(1, 0, 1)
+    fwd(1, 3, 3)
     last(1, 2, 1)
-    sq(0, 0, 0)
-    side_on(1, 1, 1)
-    fwd(1, 3, 1)
+    finish(0, 0)
+    side(2, 0)
+    turn(2, 0)
+    cra(0, 2, 1)
+    cra(0, 1, 1)
     last(1, 1, 3)
-    cra(0, 3, 0)
-    side_on(1, 1, 3)
+    finish(0, 1)
+    side(2, 1)
+    turn(2, 1)
+    cra(0, 2, 0)
+    crb(0, 2, 1)
+    crb(0, 2, 0)
+    fwd(1, 0, 3)
     fwd(1, 0, 1)
-    cra(0, 2, 0)
-    fwd(1, 0, 3)
-    last(1, 2, 3)
-    finish(0, 0)
-    turn(2, 0)
-    side(2, 0)
-    fwd(1, 3, 3)
-    last(1, 3, 1)
-    crb(0, 2, 0)
-    last(1, 1, 1)
-    finish(0, 1)
-    turn(2, 1)
-    send_far(1, 0)
-    cra(0, 1, 1)
-    last(1, 3, 3)
-    cra(0, 2, 1)
-    cra(0, 3, 1)
-    crb(0, 2, 1)
-    last(1, 0, 1)
     send_far(1, 1)
     crb(0, 1, 1)
+    last(1, 3, 3)
+    cra(0, 3, 1)
+    last(1, 3, 1)
+    own(2, 2)
+    send_far(1, 0)
+    cra(0, 3, 0)
+    cra(0, 1, 0)
     own(2, 3)
-    own(2, 2)
-    cra(0, 1, 0)
-    side(2, 1)
-    cra(0, 0, 1)
-    own(2, 1)
-    crb(0, 1, 0)
+    crb(0, 3, 1)
+    free(1, 1, 1)
+    last(1, 0, 3)
+    free(1, 1, 3)
+    dep(1, 1, 1)
+    fwd(2, 2, 3)
+    dep(1, 1, 3)
     crb(0, 3, 0)
-    free(1, 3)
-    side_on(2, 0, 1)
-    dep(1, 1)
-    side_on(2, 0, 3)
-    fwd(2, 2, 3)
-    cra(0, 0, 0)
-    fwd(2, 3, 3)
-    own(2, 0)
-    crb(0, 3, 1)
-    fwd(2, 2, 1)
-    free(1, 1)
-    fwd(2, 3, 1)
-    dep(1, 3)
-    last(1, 0, 3)
     side_on(2, 1, 3)
     side_on(2, 1, 1)
+    cra(0, 0, 1)
+    fwd(2, 2, 1)
+    side_on(2, 0, 1)
+    crb(0, 1, 0)
+    free(1, 0, 3)
+    fwd(2, 3, 3)
+    free(1, 0, 1)
+    own(2, 1)
+    dep(1, 0, 1)
+    last(1, 0, 1)
+    cra(0, 0, 0)
+    fwd(2, 3, 1)
+    own(2, 0)
+    side_on(2, 0, 3)
+    last(2, 2, 1)
+    last(2, 2, 3)
     crb(0, 0, 1)
+    dep(1, 0, 3)
+    finish(1, 1)
+    last(2, 3, 3)
+    side(3, 1)
+    turn(3, 1)
+    crb(0, 0, 0)
+    last(2, 3, 1)
     fwd(2, 1, 3)
+    sq(1, 3, 0)
+    finish(1, 0)
     fwd(2, 1, 1)
-    crb(0, 0, 0)
-    finish(1, 0)
     turn(3, 0)
-    last(2, 3, 3)
     side(3, 0)
-    last(2, 2, 3)
-    last(2, 2, 1)
+    last(2, 1, 3)
+    sq(1, 2, 1)
+    fwd(2, 0, 1)
     sq(1, 2, 0)
-    sq(1, 2, 1)
+    send_far(2, 1)
+    last(2, 1, 1)
+    own(3, 2)
+    send_far(2, 0)
+    sq(1, 1, 1)
+    dep(2, 1, 1)
+    own(3, 3)
+    free(2, 0, 3)
+    side_on(3, 0, 1)
+    side_on(3, 0, 3)
+    sq(1, 3, 1)
+    dep(2, 1, 3)
+    fwd(3, 2, 1)
+    sq(1, 1, 0)
+    fwd(3, 2, 3)
     fwd(2, 0, 3)
-    last(2, 3, 1)
-    last(2, 1, 3)
-    last(2, 1, 1)
-    finish(1, 1)
-    turn(3, 1)
-    send_far(2, 0)
-    fwd(2, 0, 1)
-    side(3, 1)
-    sq(1, 1, 1)
-    send_far(2, 1)
-    own(3, 2)
-    free(2, 1)
-    side_on(3, 0, 3)
-    sq(1, 3, 0)
-    own(3, 3)
-    side_on(3, 0, 1)
-    free(2, 3)
-    sq(1, 1, 0)
-    sq(1, 3, 1)
-    fwd(3, 2, 3)
+    free(2, 0, 1)
+    own(3, 1)
+    side_on(3, 1, 1)
     side_on(3, 1, 3)
-    dep(2, 3)
-    fwd(3, 2, 1)
-    last(2, 0, 1)
-    own(3, 1)
+    fwd(3, 3, 1)
+    dep(2, 0, 1)
+    free(2, 1, 3)
+    cra(1, 1, 0)
+    fwd(3, 3, 3)
+    last(3, 2, 3)
+    last(2, 0, 3)
     cra(1, 2, 0)
-    side_on(3, 1, 1)
-    cra(1, 1, 0)
-    dep(2, 1)
-    fwd(3, 3, 1)
+    dep(2, 0, 3)
+    last(3, 2, 1)
+    free(2, 1, 1)
+    fwd(3, 1, 1)
+    cra(1, 1, 1)
     cra(1, 3, 0)
-    last(3, 2, 1)
-    last(3, 2, 3)
-    own(3, 0)
     crb(1, 2, 0)
-    fwd(3, 3, 3)
-    fwd(3, 1, 1)
-    cra(1, 2, 1)
-    cra(1, 3, 1)
-    last(2, 0, 3)
-    crb(1, 2, 1)
-    send_far(3, 1)
     fwd(3, 1, 3)
     send_far(3, 0)
+    cra(1, 2, 1)
+    last(3, 3, 3)
+    last(2, 0, 1)
+    crb(1, 2, 1)
+    last(3, 1, 1)
+    send_far(3, 1)
+    own(3, 0)
     last(3, 3, 1)
-    cra(1, 1, 1)
-    last(3, 3, 3)
+    sq(1, 0, 0)
+    last(3, 1, 3)
+    crb(1, 3, 0)
+    crb(1, 1, 1)
+    free(3, 1, 1)
+    free(3, 0, 3)
+    dep(3, 0, 3)
+    crb(1, 1, 0)
     fwd(3, 0, 3)
-    crb(1, 3, 0)
-    last(3, 1, 1)
-    last(3, 1, 3)
+    dep(3, 0, 1)
+    cra(1, 0, 0)
+    free(3, 0, 1)
+    fwd(3, 0, 1)
+    cra(1, 3, 1)
+    crb(1, 3, 1)
+    last(3, 0, 3)
+    free(3, 1, 3)
+    finish(2, 0)
+    cra(1, 0, 1)
+    last(3, 0, 1)
+    crb(1, 0, 0)
+    dep(3, 1, 3)
+    dep(3, 1, 1)
+    finish(3, 0)
     sq(1, 0, 1)
-    free(3, 3)
-    crb(1, 3, 1)
-    crb(1, 1, 1)
-    free(3, 1)
-    fwd(3, 0, 1)
-    crb(1, 1, 0)
-    sq(1, 0, 0)
-    cra(1, 0, 0)
     finish(2, 1)
-    cra(1, 0, 1)
-    last(3, 0, 3)
-    last(3, 0, 1)
-    dep(3, 1)
-    dep(3, 3)
-    finish(2, 0)
     crb(1, 0, 1)
-    crb(1, 0, 0)
     finish(3, 1)
-    finish(3, 0)
-
+
+    got(*(name for name in moves if name[0] == "out"))
     gone(*copies)
 
 
-def hand_on(zero, first, out_zero, out_first, sem):
-    copies = []
+def hand_on(zero, first, out_zero, out_first, held, in_sem, out_sem):
+    ins, outs = [], []
     for i in range(4):
         where = pl.ds(i * SUB, SUB)
-        for src, dst in ((zero, out_zero), (first, out_first)):
-            copies.append(pltpu.make_async_copy(src.at[where], dst.at[where], sem.at[len(copies)]))
-            copies[-1].start()
-    for copy in copies:
-        copy.wait()
+        for p, (src, dst) in enumerate(((zero, out_zero), (first, out_first))):
+            n, slot = len(ins), held.at[p, where]
+            ins.append(pltpu.make_async_copy(src.at[where], slot, in_sem.at[n]))
+            outs.append(pltpu.make_async_copy(slot, dst.at[where], out_sem.at[n]))
+            ins[n].start()
+    for arrive, leave in zip(ins, outs):
+        arrive.wait()
+        leave.start()
+    for leave in outs:
+        leave.wait()
 
 
 def on_device(density, strips, dest_device, atom_slot, block_slot, patterns):
@@ -537,20 +565,21 @@
         in_specs=[
             hbm, hbm, vmem, vmem, vmem, hbm,
         ],
-        out_specs=(vmem, vmem),
+        out_specs=(hbm, hbm),
         scratch_shapes=[
             pltpu.VMEM((4, TR, KB), BF),
             pltpu.VMEM((4, 4, KB, TC), BF),
             pltpu.VMEM((2, 4, TR, TC), F32),
             pltpu.VMEM((2, 3, TR, TC), BF),
             pltpu.VMEM((4, 2, TR, TC), BF),
-            pltpu.VMEM((4, 2, HALF, TC), BF),
+            pltpu.VMEM((4, TR, TC), BF),
             pltpu.VMEM((ITEMS, WIDE), BF),
             pltpu.VMEM((2, SLOTS, WIDE), BF),
             pltpu.VMEM((2, SLOTS, WIDE), BF),
             pltpu.VMEM((TC // BLK * TR, BLK), F32),
             pltpu.VMEM((ITEMS * ATOM, BLK), BF),
             pltpu.SMEM((3, 48, 48), I32),
+            pltpu.VMEM((2, TR, TC), F32),
             pltpu.SemaphoreType.DMA((N_COPIES,)),
             pltpu.SemaphoreType.DMA((N_COPIES,)),
             pltpu.SemaphoreType.DMA((16,)),
@@ -572,7 +601,11 @@
         out_shape=(out, out),
         in_specs=(hbm, hbm),
         out_specs=(hbm, hbm),
-        scratch_shapes=[pltpu.SemaphoreType.DMA((8,))],
+        scratch_shapes=[
+            pltpu.VMEM((2, TR, TC), F32),
+            pltpu.SemaphoreType.DMA((8,)),
+            pltpu.SemaphoreType.DMA((8,)),
+        ],
     )(*results))
 
 

time: 218 us -> 147 us (0.67); the launches traced: 218 us -> 145 us
  Pallas kernels: 217 us -> 144 us
    pallas_call x1, Pallas kernels: 72.6 us -> 2.49 us  [on_device(): pl.pallas_call(hand_on, out_shape=(out, out), in_specs=(hbm, hbm), out_sp...]
    pallas_call x1, Pallas kernels: 145 us -> 141 us  [on_device(): pl.pallas_call(kernel, out_shape=(out, out), in_specs=[hbm, hbm, vmem, vm...]
where the time goes in v6:
time: 147 us; the launch traced here: 145 us
  Pallas kernels  144 us (98%)
    pallas_call x1, Pallas kernels, on_device(): pl.pallas_call(kernel, out_shape=(out, out), in_specs=[hbm, hbm, vmem, vm...  141 us

profile of v6, /device:TPU:1, one launch (start us, length us, event | category | flops | bytes accessed | tf_op | source)
XLA Modules:
  0.0 144.5 jit_solution(7430666640162625637)
XLA Ops:
  0.6 141.2 %shard_map.77 = (f32[768,384]{1,0:T(8,128)}, f32[768,384]{1,0:T(8,128)}) custom-call(bf16[768,384]{1,0:T(8,128)(2,1)} %zero_hbm.1, bf16[1024,128]{1,0:T(8,128)(2,1)} %bitcast.4, s32[1,128]{1,0:T(1,128)} %bitcast.5, s32[1,128]{1,0:T(1,128)} %bitcast.6, s32[1,128]{1,0:T(1,128)} %bitcast.7, s32[3,48,48]{2,1,0:T(8,128)} %patterns_hbm.1), custom_call_target="tpu_custom_call" | custom-call | flops 21743271936 | bytes 8388608 | tf_op jit(solution)/shard_map/pallas_call | solution.py:562
  141.8 2.5 %shard_map.78 = (f32[768,384]{1,0:T(8,128)}, f32[768,384]{1,0:T(8,128)}) custom-call(f32[768,384]{1,0:T(8,128)} %get-tuple-element.4.zero, f32[768,384]{1,0:T(8,128)} %get-tuple-element.5.first), custom_call_target="tpu_custom_call" | custom-call | tf_op jit(solution)/shard_map/pallas_call | solution.py:599

commit v7 on v6

--- a/solution.py
+++ b/solution.py
@@ -323,216 +323,216 @@
     strips_place()
     pl.semaphore_wait(barrier, len(peers))
 
+    turn(0, 0)
     strips_x()
+    side(0, 0)
     turn(0, 1)
+    own(0, 2)
+    strips_col()
     side(0, 1)
-    turn(0, 0)
-    strips_col()
-    side(0, 0)
+    side_on(0, 0, 1)
+    own(0, 0)
     own(0, 3)
-    side_on(0, 1, 1)
-    own(0, 2)
-    side_on(0, 1, 3)
-    own(0, 1)
-    fwd(0, 3, 3)
+    side_on(0, 0, 3)
     fwd(0, 2, 1)
     fwd(0, 2, 3)
+    own(0, 1)
     field()
-    own(0, 0)
+    turn(1, 1)
+    fwd(0, 0, 3)
+    fwd(0, 3, 1)
     turn(1, 0)
+    fwd(0, 0, 1)
+    fwd(0, 3, 3)
+    last(0, 2, 3)
+    side_on(0, 1, 1)
     fwd(0, 1, 1)
+    side_on(0, 1, 3)
+    side(1, 1)
+    fwd(0, 1, 3)
     last(0, 2, 1)
-    last(0, 3, 3)
-    side_on(0, 0, 3)
-    turn(1, 1)
-    fwd(0, 1, 3)
-    fwd(0, 3, 1)
-    side_on(0, 0, 1)
-    last(0, 2, 3)
-    fwd(0, 0, 1)
-    sq(0, 2, 1)
-    send_far(0, 1)
-    side(1, 1)
-    side(1, 0)
-    fwd(0, 0, 3)
-    last(0, 1, 3)
-    own(1, 2)
-    last(0, 3, 1)
-    own(1, 1)
     sq(0, 2, 0)
     send_far(0, 0)
     last(0, 1, 1)
-    sq(0, 3, 1)
-    last(0, 0, 1)
+    last(0, 3, 1)
+    own(1, 2)
+    last(0, 1, 3)
+    last(0, 3, 3)
+    side(1, 0)
+    sq(0, 2, 1)
+    send_far(0, 1)
+    own(1, 3)
+    sq(0, 1, 0)
     sq(0, 3, 0)
-    sq(0, 1, 0)
+    last(0, 0, 3)
     free(0, 0, 3)
     free(0, 0, 1)
+    own(1, 0)
+    sq(0, 3, 1)
+    dep(0, 0, 3)
+    dep(0, 0, 1)
+    last(0, 0, 1)
+    side_on(1, 1, 1)
+    sq(0, 1, 1)
+    fwd(1, 2, 1)
+    dep(0, 1, 1)
+    side_on(1, 1, 3)
+    sq(0, 0, 0)
     dep(0, 1, 3)
-    sq(0, 1, 1)
-    own(1, 3)
-    last(0, 0, 3)
-    free(0, 1, 1)
-    dep(0, 0, 1)
-    fwd(1, 1, 1)
     fwd(1, 2, 3)
-    dep(0, 0, 3)
-    fwd(1, 2, 1)
-    sq(0, 0, 0)
-    free(0, 1, 3)
-    side_on(1, 1, 3)
-    fwd(1, 1, 3)
-    side_on(1, 1, 1)
-    own(1, 0)
-    dep(0, 1, 1)
-    side_on(1, 0, 3)
-    last(1, 2, 3)
-    last(1, 1, 1)
     fwd(1, 3, 1)
     sq(0, 0, 1)
+    fwd(1, 3, 3)
+    free(0, 1, 1)
+    fwd(1, 0, 1)
+    own(1, 1)
+    side_on(1, 0, 3)
+    free(0, 1, 3)
+    finish(0, 0)
+    turn(2, 0)
+    last(1, 2, 3)
+    last(1, 2, 1)
     side_on(1, 0, 1)
-    fwd(1, 3, 3)
-    last(1, 2, 1)
-    finish(0, 0)
+    last(1, 3, 3)
     side(2, 0)
-    turn(2, 0)
     cra(0, 2, 1)
+    crb(0, 2, 1)
     cra(0, 1, 1)
+    last(1, 3, 1)
+    send_far(1, 1)
+    fwd(1, 1, 3)
+    fwd(1, 1, 1)
+    finish(0, 1)
+    turn(2, 1)
+    fwd(1, 0, 3)
+    cra(0, 1, 0)
+    cra(0, 2, 0)
+    crb(0, 2, 0)
+    send_far(1, 0)
+    side(2, 1)
     last(1, 1, 3)
-    finish(0, 1)
-    side(2, 1)
-    turn(2, 1)
-    cra(0, 2, 0)
-    crb(0, 2, 1)
-    crb(0, 2, 0)
-    fwd(1, 0, 3)
-    fwd(1, 0, 1)
-    send_far(1, 1)
+    cra(0, 3, 1)
+    last(1, 1, 1)
+    crb(0, 3, 1)
     crb(0, 1, 1)
-    last(1, 3, 3)
-    cra(0, 3, 1)
-    last(1, 3, 1)
-    own(2, 2)
-    send_far(1, 0)
-    cra(0, 3, 0)
-    cra(0, 1, 0)
-    own(2, 3)
-    crb(0, 3, 1)
-    free(1, 1, 1)
-    last(1, 0, 3)
+    cra(0, 0, 0)
     free(1, 1, 3)
     dep(1, 1, 1)
-    fwd(2, 2, 3)
+    own(2, 2)
     dep(1, 1, 3)
-    crb(0, 3, 0)
-    side_on(2, 1, 3)
-    side_on(2, 1, 1)
     cra(0, 0, 1)
-    fwd(2, 2, 1)
+    cra(0, 3, 0)
+    last(1, 0, 3)
+    own(2, 1)
+    free(1, 1, 1)
     side_on(2, 0, 1)
     crb(0, 1, 0)
+    side_on(2, 1, 3)
+    free(1, 0, 1)
+    crb(0, 3, 0)
+    last(1, 0, 1)
     free(1, 0, 3)
+    side_on(2, 0, 3)
+    dep(1, 0, 1)
+    dep(1, 0, 3)
+    own(2, 3)
+    fwd(2, 2, 1)
+    fwd(2, 2, 3)
+    crb(0, 0, 1)
+    side_on(2, 1, 1)
+    fwd(2, 1, 3)
+    finish(1, 1)
+    turn(3, 1)
+    side(3, 1)
+    fwd(2, 1, 1)
+    crb(0, 0, 0)
+    last(2, 2, 3)
     fwd(2, 3, 3)
-    free(1, 0, 1)
-    own(2, 1)
-    dep(1, 0, 1)
-    last(1, 0, 1)
-    cra(0, 0, 0)
+    own(2, 0)
+    last(2, 2, 1)
+    last(2, 1, 1)
+    last(2, 1, 3)
+    finish(1, 0)
+    turn(3, 0)
     fwd(2, 3, 1)
-    own(2, 0)
-    side_on(2, 0, 3)
-    last(2, 2, 1)
-    last(2, 2, 3)
-    crb(0, 0, 1)
-    dep(1, 0, 3)
-    finish(1, 1)
+    sq(1, 2, 0)
+    sq(1, 1, 1)
+    send_far(2, 0)
+    side(3, 0)
+    side_on(3, 1, 3)
+    sq(1, 1, 0)
+    sq(1, 2, 1)
     last(2, 3, 3)
-    side(3, 1)
-    turn(3, 1)
-    crb(0, 0, 0)
     last(2, 3, 1)
-    fwd(2, 1, 3)
+    send_far(2, 1)
+    own(3, 2)
+    sq(1, 3, 1)
     sq(1, 3, 0)
-    finish(1, 0)
-    fwd(2, 1, 1)
-    turn(3, 0)
-    side(3, 0)
-    last(2, 1, 3)
-    sq(1, 2, 1)
-    fwd(2, 0, 1)
-    sq(1, 2, 0)
-    send_far(2, 1)
-    last(2, 1, 1)
-    own(3, 2)
-    send_far(2, 0)
-    sq(1, 1, 1)
+    free(2, 0, 3)
+    free(2, 0, 1)
+    free(2, 1, 3)
+    own(3, 3)
+    dep(2, 0, 1)
+    free(2, 1, 1)
+    side_on(3, 1, 1)
+    fwd(3, 2, 1)
+    dep(2, 0, 3)
+    fwd(3, 2, 3)
+    own(3, 1)
+    fwd(2, 0, 3)
     dep(2, 1, 1)
-    own(3, 3)
-    free(2, 0, 3)
     side_on(3, 0, 1)
     side_on(3, 0, 3)
-    sq(1, 3, 1)
     dep(2, 1, 3)
-    fwd(3, 2, 1)
-    sq(1, 1, 0)
-    fwd(3, 2, 3)
-    fwd(2, 0, 3)
-    free(2, 0, 1)
-    own(3, 1)
-    side_on(3, 1, 1)
-    side_on(3, 1, 3)
+    cra(1, 2, 1)
+    last(3, 2, 3)
     fwd(3, 3, 1)
-    dep(2, 0, 1)
-    free(2, 1, 3)
+    cra(1, 3, 1)
+    last(3, 2, 1)
+    cra(1, 1, 1)
+    fwd(3, 3, 3)
+    crb(1, 2, 1)
+    fwd(3, 1, 1)
+    fwd(3, 1, 3)
+    own(3, 0)
     cra(1, 1, 0)
-    fwd(3, 3, 3)
-    last(3, 2, 3)
+    send_far(3, 1)
+    cra(1, 2, 0)
+    cra(1, 3, 0)
+    last(3, 3, 1)
+    last(3, 3, 3)
+    crb(1, 2, 0)
+    last(3, 1, 3)
+    fwd(2, 0, 1)
+    last(3, 1, 1)
+    send_far(3, 0)
     last(2, 0, 3)
-    cra(1, 2, 0)
-    dep(2, 0, 3)
-    last(3, 2, 1)
-    free(2, 1, 1)
-    fwd(3, 1, 1)
-    cra(1, 1, 1)
-    cra(1, 3, 0)
-    crb(1, 2, 0)
-    fwd(3, 1, 3)
-    send_far(3, 0)
-    cra(1, 2, 1)
-    last(3, 3, 3)
+    crb(1, 3, 1)
+    free(3, 1, 3)
+    crb(1, 1, 0)
+    fwd(3, 0, 3)
+    free(3, 0, 1)
+    crb(1, 3, 0)
+    free(3, 0, 3)
     last(2, 0, 1)
-    crb(1, 2, 1)
-    last(3, 1, 1)
-    send_far(3, 1)
-    own(3, 0)
-    last(3, 3, 1)
-    sq(1, 0, 0)
-    last(3, 1, 3)
-    crb(1, 3, 0)
     crb(1, 1, 1)
     free(3, 1, 1)
-    free(3, 0, 3)
     dep(3, 0, 3)
-    crb(1, 1, 0)
-    fwd(3, 0, 3)
+    sq(1, 0, 1)
+    cra(1, 0, 0)
+    dep(3, 1, 3)
+    fwd(3, 0, 1)
     dep(3, 0, 1)
-    cra(1, 0, 0)
-    free(3, 0, 1)
-    fwd(3, 0, 1)
-    cra(1, 3, 1)
-    crb(1, 3, 1)
+    finish(2, 1)
+    cra(1, 0, 1)
     last(3, 0, 3)
-    free(3, 1, 3)
+    dep(3, 1, 1)
+    sq(1, 0, 0)
     finish(2, 0)
-    cra(1, 0, 1)
     last(3, 0, 1)
+    crb(1, 0, 1)
     crb(1, 0, 0)
-    dep(3, 1, 3)
-    dep(3, 1, 1)
     finish(3, 0)
-    sq(1, 0, 1)
-    finish(2, 1)
-    crb(1, 0, 1)
     finish(3, 1)
 
     got(*(name for name in moves if name[0] == "out"))

time: 147 us -> 141 us (0.959); the launches traced: 145 us -> 141 us
  Pallas kernels: 144 us -> 140 us
    pallas_call x1, Pallas kernels: 141 us -> 137 us  [on_device(): pl.pallas_call(kernel, out_shape=(out, out), in_specs=[hbm, hbm, vmem, vm...]
where the time goes in v7:
time: 141 us
  Pallas kernels  140 us (99%)
    pallas_call x1, Pallas kernels, on_device(): pl.pallas_call(kernel, out_shape=(out, out), in_specs=[hbm, hbm, vmem, vm...  137 us

profile of v7, /device:TPU:1, one launch (start us, length us, event | category | flops | bytes accessed | tf_op | source)
XLA Modules:
  0.0 140.7 jit_solution(9136947146543355407)
XLA Ops:
  0.6 137.4 %shard_map.77 = (f32[768,384]{1,0:T(8,128)}, f32[768,384]{1,0:T(8,128)}) custom-call(bf16[768,384]{1,0:T(8,128)(2,1)} %zero_hbm.1, bf16[1024,128]{1,0:T(8,128)(2,1)} %bitcast.4, s32[1,128]{1,0:T(1,128)} %bitcast.5, s32[1,128]{1,0:T(1,128)} %bitcast.6, s32[1,128]{1,0:T(1,128)} %bitcast.7, s32[3,48,48]{2,1,0:T(8,128)} %patterns_hbm.1), custom_call_target="tpu_custom_call" | custom-call | flops 21743271936 | bytes 8388608 | tf_op jit(solution)/shard_map/pallas_call | solution.py:562
  138.0 2.5 %shard_map.78 = (f32[768,384]{1,0:T(8,128)}, f32[768,384]{1,0:T(8,128)}) custom-call(f32[768,384]{1,0:T(8,128)} %get-tuple-element.4.zero, f32[768,384]{1,0:T(8,128)} %get-tuple-element.5.first), custom_call_target="tpu_custom_call" | custom-call | tf_op jit(solution)/shard_map/pallas_call | solution.py:599

commit v8 on v7

--- a/solution.py
+++ b/solution.py
@@ -323,217 +323,217 @@
     strips_place()
     pl.semaphore_wait(barrier, len(peers))
 
+    side(0, 0)
     turn(0, 0)
+    side(0, 1)
+    turn(0, 1)
     strips_x()
-    side(0, 0)
-    turn(0, 1)
     own(0, 2)
+    own(0, 1)
     strips_col()
-    side(0, 1)
-    side_on(0, 0, 1)
-    own(0, 0)
+    fwd(0, 2, 1)
+    side_on(0, 1, 3)
     own(0, 3)
     side_on(0, 0, 3)
-    fwd(0, 2, 1)
+    side_on(0, 1, 1)
     fwd(0, 2, 3)
-    own(0, 1)
+    fwd(0, 1, 1)
+    last(0, 2, 1)
+    own(0, 0)
+    side_on(0, 0, 1)
     field()
-    turn(1, 1)
-    fwd(0, 0, 3)
-    fwd(0, 3, 1)
     turn(1, 0)
-    fwd(0, 0, 1)
+    side(1, 1)
+    last(0, 1, 1)
     fwd(0, 3, 3)
     last(0, 2, 3)
-    side_on(0, 1, 1)
-    fwd(0, 1, 1)
-    side_on(0, 1, 3)
-    side(1, 1)
+    fwd(0, 0, 3)
     fwd(0, 1, 3)
-    last(0, 2, 1)
-    sq(0, 2, 0)
-    send_far(0, 0)
-    last(0, 1, 1)
-    last(0, 3, 1)
-    own(1, 2)
-    last(0, 1, 3)
-    last(0, 3, 3)
+    fwd(0, 3, 1)
+    turn(1, 1)
     side(1, 0)
     sq(0, 2, 1)
     send_far(0, 1)
-    own(1, 3)
-    sq(0, 1, 0)
+    fwd(0, 0, 1)
+    sq(0, 2, 0)
+    send_far(0, 0)
+    last(0, 3, 3)
+    last(0, 3, 1)
+    sq(0, 3, 1)
+    last(0, 1, 3)
+    own(1, 2)
+    free(0, 1, 3)
     sq(0, 3, 0)
-    last(0, 0, 3)
-    free(0, 0, 3)
-    free(0, 0, 1)
-    own(1, 0)
-    sq(0, 3, 1)
-    dep(0, 0, 3)
-    dep(0, 0, 1)
-    last(0, 0, 1)
+    side_on(1, 1, 3)
     side_on(1, 1, 1)
     sq(0, 1, 1)
+    free(0, 1, 1)
+    own(1, 1)
+    dep(0, 1, 1)
+    last(0, 0, 3)
+    sq(0, 1, 0)
+    own(1, 3)
+    dep(0, 1, 3)
+    free(0, 0, 1)
+    dep(0, 0, 1)
+    side_on(1, 0, 3)
     fwd(1, 2, 1)
-    dep(0, 1, 1)
-    side_on(1, 1, 3)
+    free(0, 0, 3)
+    fwd(1, 2, 3)
+    last(0, 0, 1)
+    own(1, 0)
+    dep(0, 0, 3)
     sq(0, 0, 0)
-    dep(0, 1, 3)
-    fwd(1, 2, 3)
+    side_on(1, 0, 1)
+    fwd(1, 1, 1)
+    sq(0, 0, 1)
+    cra(0, 1, 1)
+    finish(0, 1)
+    fwd(1, 1, 3)
+    cra(0, 3, 1)
+    side(2, 1)
+    turn(2, 1)
+    last(1, 2, 1)
+    last(1, 2, 3)
+    fwd(1, 3, 3)
+    cra(0, 2, 1)
+    crb(0, 2, 1)
+    send_far(1, 1)
+    cra(0, 2, 0)
     fwd(1, 3, 1)
-    sq(0, 0, 1)
-    fwd(1, 3, 3)
-    free(0, 1, 1)
-    fwd(1, 0, 1)
-    own(1, 1)
-    side_on(1, 0, 3)
-    free(0, 1, 3)
+    last(1, 3, 3)
     finish(0, 0)
     turn(2, 0)
-    last(1, 2, 3)
-    last(1, 2, 1)
-    side_on(1, 0, 1)
-    last(1, 3, 3)
+    last(1, 1, 1)
+    last(1, 1, 3)
+    fwd(1, 0, 3)
     side(2, 0)
-    cra(0, 2, 1)
-    crb(0, 2, 1)
-    cra(0, 1, 1)
+    crb(0, 2, 0)
+    crb(0, 1, 1)
     last(1, 3, 1)
-    send_far(1, 1)
-    fwd(1, 1, 3)
-    fwd(1, 1, 1)
-    finish(0, 1)
-    turn(2, 1)
-    fwd(1, 0, 3)
+    free(1, 1, 1)
+    send_far(1, 0)
+    side_on(2, 1, 1)
     cra(0, 1, 0)
-    cra(0, 2, 0)
-    crb(0, 2, 0)
-    send_far(1, 0)
-    side(2, 1)
-    last(1, 1, 3)
-    cra(0, 3, 1)
-    last(1, 1, 1)
+    fwd(1, 0, 1)
     crb(0, 3, 1)
-    crb(0, 1, 1)
-    cra(0, 0, 0)
-    free(1, 1, 3)
-    dep(1, 1, 1)
-    own(2, 2)
     dep(1, 1, 3)
-    cra(0, 0, 1)
-    cra(0, 3, 0)
     last(1, 0, 3)
     own(2, 1)
-    free(1, 1, 1)
+    own(2, 2)
+    free(1, 1, 3)
+    crb(0, 1, 0)
+    dep(1, 1, 1)
+    cra(0, 3, 0)
     side_on(2, 0, 1)
-    crb(0, 1, 0)
-    side_on(2, 1, 3)
-    free(1, 0, 1)
+    last(1, 0, 1)
     crb(0, 3, 0)
-    last(1, 0, 1)
+    own(2, 3)
     free(1, 0, 3)
     side_on(2, 0, 3)
+    dep(1, 0, 3)
+    free(1, 0, 1)
+    cra(0, 0, 1)
+    crb(0, 0, 1)
+    fwd(2, 1, 1)
+    side_on(2, 1, 3)
     dep(1, 0, 1)
-    dep(1, 0, 3)
-    own(2, 3)
+    fwd(2, 2, 3)
+    finish(1, 1)
     fwd(2, 2, 1)
-    fwd(2, 2, 3)
-    crb(0, 0, 1)
-    side_on(2, 1, 1)
+    side(3, 1)
     fwd(2, 1, 3)
-    finish(1, 1)
+    cra(0, 0, 0)
     turn(3, 1)
-    side(3, 1)
-    fwd(2, 1, 1)
+    fwd(2, 3, 1)
     crb(0, 0, 0)
+    fwd(2, 3, 3)
+    last(2, 1, 1)
+    own(2, 0)
     last(2, 2, 3)
-    fwd(2, 3, 3)
-    own(2, 0)
     last(2, 2, 1)
-    last(2, 1, 1)
-    last(2, 1, 3)
     finish(1, 0)
     turn(3, 0)
-    fwd(2, 3, 1)
+    last(2, 1, 3)
+    sq(1, 2, 1)
+    side(3, 0)
+    send_far(2, 1)
+    sq(1, 1, 0)
+    last(2, 3, 1)
     sq(1, 2, 0)
+    last(2, 3, 3)
+    fwd(2, 0, 1)
+    send_far(2, 0)
+    side_on(3, 1, 1)
     sq(1, 1, 1)
-    send_far(2, 0)
-    side(3, 0)
-    side_on(3, 1, 3)
-    sq(1, 1, 0)
-    sq(1, 2, 1)
-    last(2, 3, 3)
-    last(2, 3, 1)
-    send_far(2, 1)
     own(3, 2)
     sq(1, 3, 1)
+    side_on(3, 1, 3)
     sq(1, 3, 0)
-    free(2, 0, 3)
-    free(2, 0, 1)
     free(2, 1, 3)
     own(3, 3)
-    dep(2, 0, 1)
     free(2, 1, 1)
-    side_on(3, 1, 1)
-    fwd(3, 2, 1)
-    dep(2, 0, 3)
-    fwd(3, 2, 3)
-    own(3, 1)
-    fwd(2, 0, 3)
+    side_on(3, 0, 3)
+    dep(2, 1, 3)
     dep(2, 1, 1)
     side_on(3, 0, 1)
-    side_on(3, 0, 3)
-    dep(2, 1, 3)
+    fwd(3, 2, 1)
+    fwd(3, 2, 3)
+    free(2, 0, 1)
+    dep(2, 0, 1)
+    free(2, 0, 3)
+    own(3, 1)
+    dep(2, 0, 3)
     cra(1, 2, 1)
+    fwd(3, 3, 3)
+    cra(1, 3, 1)
+    last(3, 2, 1)
     last(3, 2, 3)
     fwd(3, 3, 1)
-    cra(1, 3, 1)
-    last(3, 2, 1)
+    cra(1, 2, 0)
+    fwd(2, 0, 3)
+    crb(1, 2, 1)
+    send_far(3, 1)
+    fwd(3, 1, 3)
+    fwd(3, 1, 1)
+    cra(1, 1, 0)
+    own(3, 0)
+    last(3, 3, 3)
+    last(3, 3, 1)
+    last(2, 0, 1)
+    crb(1, 2, 0)
+    send_far(3, 0)
+    crb(1, 3, 1)
+    last(3, 1, 1)
+    last(3, 1, 3)
     cra(1, 1, 1)
-    fwd(3, 3, 3)
-    crb(1, 2, 1)
-    fwd(3, 1, 1)
-    fwd(3, 1, 3)
-    own(3, 0)
-    cra(1, 1, 0)
-    send_far(3, 1)
-    cra(1, 2, 0)
-    cra(1, 3, 0)
-    last(3, 3, 1)
-    last(3, 3, 3)
-    crb(1, 2, 0)
-    last(3, 1, 3)
-    fwd(2, 0, 1)
-    last(3, 1, 1)
-    send_far(3, 0)
-    last(2, 0, 3)
-    crb(1, 3, 1)
-    free(3, 1, 3)
-    crb(1, 1, 0)
-    fwd(3, 0, 3)
-    free(3, 0, 1)
-    crb(1, 3, 0)
-    free(3, 0, 3)
-    last(2, 0, 1)
     crb(1, 1, 1)
     free(3, 1, 1)
+    free(3, 1, 3)
+    fwd(3, 0, 1)
+    dep(3, 1, 3)
+    fwd(3, 0, 3)
+    last(2, 0, 3)
+    dep(3, 1, 1)
+    cra(1, 3, 0)
+    crb(1, 3, 0)
     dep(3, 0, 3)
+    crb(1, 1, 0)
+    free(3, 0, 3)
+    dep(3, 0, 1)
+    sq(1, 0, 0)
+    cra(1, 0, 1)
     sq(1, 0, 1)
+    free(3, 0, 1)
+    last(3, 0, 1)
+    finish(2, 1)
+    last(3, 0, 3)
     cra(1, 0, 0)
-    dep(3, 1, 3)
-    fwd(3, 0, 1)
-    dep(3, 0, 1)
-    finish(2, 1)
-    cra(1, 0, 1)
-    last(3, 0, 3)
-    dep(3, 1, 1)
-    sq(1, 0, 0)
+    crb(1, 0, 0)
+    crb(1, 0, 1)
+    finish(3, 1)
     finish(2, 0)
-    last(3, 0, 1)
-    crb(1, 0, 1)
-    crb(1, 0, 0)
     finish(3, 0)
-    finish(3, 1)
 
     got(*(name for name in moves if name[0] == "out"))
     gone(*copies)

time: 141 us -> 146 us (1.035); the launches traced: 141 us -> 144 us
  Pallas kernels: 140 us -> 143 us
    pallas_call x1, Pallas kernels: 137 us -> 141 us  [on_device(): pl.pallas_call(kernel, out_shape=(out, out), in_specs=[hbm, hbm, vmem, vm...]
where the time goes in v8:
time: 146 us; the launch traced here: 144 us
  Pallas kernels  143 us (98%)
    pallas_call x1, Pallas kernels, on_device(): pl.pallas_call(kernel, out_shape=(out, out), in_specs=[hbm, hbm, vmem, vm...  141 us

profile of v8, /device:TPU:1, one launch (start us, length us, event | category | flops | bytes accessed | tf_op | source)
XLA Modules:
  0.0 144.1 jit_solution(7428808815699147498)
XLA Ops:
  0.6 140.8 %shard_map.77 = (f32[768,384]{1,0:T(8,128)}, f32[768,384]{1,0:T(8,128)}) custom-call(bf16[768,384]{1,0:T(8,128)(2,1)} %zero_hbm.1, bf16[1024,128]{1,0:T(8,128)(2,1)} %bitcast.4, s32[1,128]{1,0:T(1,128)} %bitcast.5, s32[1,128]{1,0:T(1,128)} %bitcast.6, s32[1,128]{1,0:T(1,128)} %bitcast.7, s32[3,48,48]{2,1,0:T(8,128)} %patterns_hbm.1), custom_call_target="tpu_custom_call" | custom-call | flops 21743271936 | bytes 8388608 | tf_op jit(solution)/shard_map/pallas_call | solution.py:562
  141.4 2.5 %shard_map.78 = (f32[768,384]{1,0:T(8,128)}, f32[768,384]{1,0:T(8,128)}) custom-call(f32[768,384]{1,0:T(8,128)} %get-tuple-element.4.zero, f32[768,384]{1,0:T(8,128)} %get-tuple-element.5.first), custom_call_target="tpu_custom_call" | custom-call | tf_op jit(solution)/shard_map/pallas_call | solution.py:599

commit v9 on v7

--- a/solution.py
+++ b/solution.py
@@ -323,217 +323,217 @@
     strips_place()
     pl.semaphore_wait(barrier, len(peers))
 
+    side(0, 0)
     turn(0, 0)
+    turn(0, 1)
     strips_x()
-    side(0, 0)
-    turn(0, 1)
+    side(0, 1)
     own(0, 2)
     strips_col()
-    side(0, 1)
-    side_on(0, 0, 1)
-    own(0, 0)
     own(0, 3)
     side_on(0, 0, 3)
+    own(0, 1)
+    side_on(0, 1, 3)
+    fwd(0, 2, 3)
+    side_on(0, 0, 1)
+    fwd(0, 3, 3)
+    fwd(0, 3, 1)
+    side_on(0, 1, 1)
     fwd(0, 2, 1)
-    fwd(0, 2, 3)
-    own(0, 1)
+    own(0, 0)
     field()
+    turn(1, 0)
+    last(0, 2, 3)
     turn(1, 1)
+    last(0, 2, 1)
+    fwd(0, 1, 3)
+    last(0, 3, 1)
+    side(1, 0)
+    fwd(0, 1, 1)
     fwd(0, 0, 3)
-    fwd(0, 3, 1)
-    turn(1, 0)
-    fwd(0, 0, 1)
-    fwd(0, 3, 3)
-    last(0, 2, 3)
-    side_on(0, 1, 1)
-    fwd(0, 1, 1)
-    side_on(0, 1, 3)
-    side(1, 1)
-    fwd(0, 1, 3)
-    last(0, 2, 1)
     sq(0, 2, 0)
     send_far(0, 0)
+    last(0, 3, 3)
+    sq(0, 3, 0)
+    free(0, 0, 3)
+    side(1, 1)
+    fwd(0, 0, 1)
     last(0, 1, 1)
-    last(0, 3, 1)
-    own(1, 2)
-    last(0, 1, 3)
-    last(0, 3, 3)
-    side(1, 0)
     sq(0, 2, 1)
     send_far(0, 1)
     own(1, 3)
+    own(1, 2)
+    last(0, 1, 3)
     sq(0, 1, 0)
-    sq(0, 3, 0)
+    free(0, 0, 1)
+    side_on(1, 0, 3)
+    dep(0, 0, 3)
+    sq(0, 3, 1)
+    own(1, 1)
     last(0, 0, 3)
-    free(0, 0, 3)
-    free(0, 0, 1)
-    own(1, 0)
-    sq(0, 3, 1)
-    dep(0, 0, 3)
     dep(0, 0, 1)
+    sq(0, 1, 1)
+    side_on(1, 0, 1)
+    free(0, 1, 1)
     last(0, 0, 1)
     side_on(1, 1, 1)
-    sq(0, 1, 1)
+    sq(0, 0, 1)
     fwd(1, 2, 1)
+    fwd(1, 2, 3)
+    dep(0, 1, 3)
+    side_on(1, 1, 3)
+    fwd(1, 3, 3)
+    fwd(1, 3, 1)
+    free(0, 1, 3)
+    sq(0, 0, 0)
     dep(0, 1, 1)
-    side_on(1, 1, 3)
-    sq(0, 0, 0)
-    dep(0, 1, 3)
-    fwd(1, 2, 3)
-    fwd(1, 3, 1)
-    sq(0, 0, 1)
-    fwd(1, 3, 3)
-    free(0, 1, 1)
-    fwd(1, 0, 1)
-    own(1, 1)
-    side_on(1, 0, 3)
-    free(0, 1, 3)
     finish(0, 0)
+    side(2, 0)
     turn(2, 0)
     last(1, 2, 3)
+    cra(0, 1, 0)
+    own(1, 0)
+    cra(0, 2, 0)
     last(1, 2, 1)
-    side_on(1, 0, 1)
+    fwd(1, 1, 1)
+    crb(0, 2, 0)
+    last(1, 3, 1)
+    send_far(1, 0)
+    cra(0, 3, 0)
+    fwd(1, 1, 3)
+    finish(0, 1)
+    side(2, 1)
+    cra(0, 2, 1)
+    fwd(1, 0, 1)
+    turn(2, 1)
     last(1, 3, 3)
-    side(2, 0)
-    cra(0, 2, 1)
     crb(0, 2, 1)
-    cra(0, 1, 1)
-    last(1, 3, 1)
+    last(1, 1, 1)
     send_far(1, 1)
-    fwd(1, 1, 3)
-    fwd(1, 1, 1)
-    finish(0, 1)
-    turn(2, 1)
-    fwd(1, 0, 3)
-    cra(0, 1, 0)
-    cra(0, 2, 0)
-    crb(0, 2, 0)
-    send_far(1, 0)
-    side(2, 1)
     last(1, 1, 3)
     cra(0, 3, 1)
-    last(1, 1, 1)
+    crb(0, 1, 0)
+    free(1, 0, 1)
+    fwd(1, 0, 3)
+    crb(0, 3, 0)
+    dep(1, 0, 3)
+    cra(0, 1, 1)
+    own(2, 2)
+    side_on(2, 0, 3)
+    dep(1, 0, 1)
     crb(0, 3, 1)
-    crb(0, 1, 1)
-    cra(0, 0, 0)
-    free(1, 1, 3)
-    dep(1, 1, 1)
-    own(2, 2)
-    dep(1, 1, 3)
-    cra(0, 0, 1)
-    cra(0, 3, 0)
-    last(1, 0, 3)
-    own(2, 1)
-    free(1, 1, 1)
-    side_on(2, 0, 1)
-    crb(0, 1, 0)
-    side_on(2, 1, 3)
-    free(1, 0, 1)
-    crb(0, 3, 0)
     last(1, 0, 1)
     free(1, 0, 3)
-    side_on(2, 0, 3)
-    dep(1, 0, 1)
-    dep(1, 0, 3)
+    side_on(2, 1, 3)
+    side_on(2, 1, 1)
+    cra(0, 0, 0)
+    own(2, 1)
+    last(1, 0, 3)
+    crb(0, 1, 1)
+    free(1, 1, 1)
+    dep(1, 1, 1)
+    side_on(2, 0, 1)
+    fwd(2, 2, 1)
     own(2, 3)
-    fwd(2, 2, 1)
+    free(1, 1, 3)
+    dep(1, 1, 3)
+    crb(0, 0, 0)
+    finish(1, 0)
     fwd(2, 2, 3)
+    side(3, 0)
+    cra(0, 0, 1)
+    turn(3, 0)
+    fwd(2, 1, 3)
     crb(0, 0, 1)
-    side_on(2, 1, 1)
-    fwd(2, 1, 3)
+    fwd(2, 1, 1)
+    fwd(2, 3, 1)
+    fwd(2, 3, 3)
+    last(2, 2, 1)
+    last(2, 2, 3)
     finish(1, 1)
     turn(3, 1)
     side(3, 1)
-    fwd(2, 1, 1)
-    crb(0, 0, 0)
-    last(2, 2, 3)
-    fwd(2, 3, 3)
+    sq(1, 2, 0)
+    send_far(2, 0)
+    last(2, 1, 3)
+    sq(1, 2, 1)
     own(2, 0)
-    last(2, 2, 1)
+    side_on(3, 0, 1)
+    send_far(2, 1)
+    last(2, 3, 1)
+    side_on(3, 0, 3)
+    last(2, 3, 3)
+    sq(1, 3, 1)
+    free(2, 1, 3)
     last(2, 1, 1)
-    last(2, 1, 3)
-    finish(1, 0)
-    turn(3, 0)
-    fwd(2, 3, 1)
-    sq(1, 2, 0)
+    own(3, 2)
+    own(3, 3)
+    sq(1, 1, 0)
+    dep(2, 0, 1)
     sq(1, 1, 1)
-    send_far(2, 0)
-    side(3, 0)
     side_on(3, 1, 3)
-    sq(1, 1, 0)
-    sq(1, 2, 1)
-    last(2, 3, 3)
-    last(2, 3, 1)
-    send_far(2, 1)
-    own(3, 2)
-    sq(1, 3, 1)
+    side_on(3, 1, 1)
     sq(1, 3, 0)
+    dep(2, 0, 3)
     free(2, 0, 3)
     free(2, 0, 1)
-    free(2, 1, 3)
-    own(3, 3)
-    dep(2, 0, 1)
+    fwd(3, 2, 3)
+    fwd(3, 2, 1)
+    dep(2, 1, 1)
+    own(3, 1)
+    dep(2, 1, 3)
+    cra(1, 2, 0)
+    cra(1, 1, 0)
+    fwd(3, 3, 1)
+    last(3, 2, 1)
     free(2, 1, 1)
-    side_on(3, 1, 1)
-    fwd(3, 2, 1)
-    dep(2, 0, 3)
-    fwd(3, 2, 3)
-    own(3, 1)
-    fwd(2, 0, 3)
-    dep(2, 1, 1)
-    side_on(3, 0, 1)
-    side_on(3, 0, 3)
-    dep(2, 1, 3)
-    cra(1, 2, 1)
-    last(3, 2, 3)
-    fwd(3, 3, 1)
-    cra(1, 3, 1)
-    last(3, 2, 1)
     cra(1, 1, 1)
     fwd(3, 3, 3)
-    crb(1, 2, 1)
+    last(3, 2, 3)
+    fwd(2, 0, 1)
+    cra(1, 2, 1)
+    cra(1, 3, 1)
     fwd(3, 1, 1)
     fwd(3, 1, 3)
+    fwd(2, 0, 3)
+    crb(1, 2, 1)
+    send_far(3, 1)
     own(3, 0)
-    cra(1, 1, 0)
-    send_far(3, 1)
-    cra(1, 2, 0)
     cra(1, 3, 0)
     last(3, 3, 1)
+    crb(1, 2, 0)
+    last(3, 1, 1)
     last(3, 3, 3)
-    crb(1, 2, 0)
+    send_far(3, 0)
     last(3, 1, 3)
-    fwd(2, 0, 1)
-    last(3, 1, 1)
-    send_far(3, 0)
+    crb(1, 3, 1)
     last(2, 0, 3)
-    crb(1, 3, 1)
-    free(3, 1, 3)
-    crb(1, 1, 0)
-    fwd(3, 0, 3)
-    free(3, 0, 1)
-    crb(1, 3, 0)
-    free(3, 0, 3)
-    last(2, 0, 1)
     crb(1, 1, 1)
     free(3, 1, 1)
+    free(3, 1, 3)
+    crb(1, 3, 0)
+    fwd(3, 0, 1)
+    free(3, 0, 3)
+    fwd(3, 0, 3)
+    last(2, 0, 1)
+    dep(3, 1, 1)
+    crb(1, 1, 0)
+    dep(3, 1, 3)
+    sq(1, 0, 0)
+    cra(1, 0, 1)
+    dep(3, 0, 1)
+    free(3, 0, 1)
     dep(3, 0, 3)
     sq(1, 0, 1)
+    finish(2, 1)
     cra(1, 0, 0)
-    dep(3, 1, 3)
-    fwd(3, 0, 1)
-    dep(3, 0, 1)
-    finish(2, 1)
-    cra(1, 0, 1)
+    last(3, 0, 1)
     last(3, 0, 3)
-    dep(3, 1, 1)
-    sq(1, 0, 0)
-    finish(2, 0)
-    last(3, 0, 1)
     crb(1, 0, 1)
     crb(1, 0, 0)
+    finish(2, 0)
+    finish(3, 1)
     finish(3, 0)
-    finish(3, 1)
 
     got(*(name for name in moves if name[0] == "out"))
     gone(*copies)

time: 141 us -> 141 us (level)
  no operation moved by 1% of the time
where the time goes in v9:
time: 141 us
  Pallas kernels  140 us (99%)
    pallas_call x1, Pallas kernels, on_device(): pl.pallas_call(kernel, out_shape=(out, out), in_specs=[hbm, hbm, vmem, vm...  137 us

profile of v9, /device:TPU:1, one launch (start us, length us, event | category | flops | bytes accessed | tf_op | source)
XLA Modules:
  0.0 140.6 jit_solution(17078623513035078903)
XLA Ops:
  0.6 137.2 %shard_map.77 = (f32[768,384]{1,0:T(8,128)}, f32[768,384]{1,0:T(8,128)}) custom-call(bf16[768,384]{1,0:T(8,128)(2,1)} %zero_hbm.1, bf16[1024,128]{1,0:T(8,128)(2,1)} %bitcast.4, s32[1,128]{1,0:T(1,128)} %bitcast.5, s32[1,128]{1,0:T(1,128)} %bitcast.6, s32[1,128]{1,0:T(1,128)} %bitcast.7, s32[3,48,48]{2,1,0:T(8,128)} %patterns_hbm.1), custom_call_target="tpu_custom_call" | custom-call | flops 21743271936 | bytes 8388608 | tf_op jit(solution)/shard_map/pallas_call | solution.py:562
  137.9 2.5 %shard_map.78 = (f32[768,384]{1,0:T(8,128)}, f32[768,384]{1,0:T(8,128)}) custom-call(f32[768,384]{1,0:T(8,128)} %get-tuple-element.4.zero, f32[768,384]{1,0:T(8,128)} %get-tuple-element.5.first), custom_call_target="tpu_custom_call" | custom-call | tf_op jit(solution)/shard_map/pallas_call | solution.py:599
